TPU v7x, 256 devices: a whole 4x4x8 slice. The times are simulated.
256 devices in a mesh: grp: 4 (over y), blk: 64 (over z, x, core).
Axes of the slice: x: 4, y: 4, z: 8, core: 2. Of those that a mesh axis runs over, the one named last changes fastest.
Arguments:
- adjoint_init: float32 [5, 128, 65536], P(None, 'grp', 'blk'), may hold values from -6 to 6
- adjoint_rhs: float32 [5, 128, 65536], P(None, 'grp', 'blk'), may hold values from -24 to 24
- flow_state: float32 [5, 128, 65536], P(None, 'grp', 'blk'), may hold values from -2 to 8, as said below
- face_weights: bfloat16 [6, 128, 65536], P(None, 'grp', 'blk'), may hold values from 0.29882812 to 1.1953125
- pseudo_time: float32 [128, 65536], P('grp', 'blk'), may hold values from 1 to 4
- tet_coords: float32 [4, 3, 524288], P(None, None, ('grp', 'blk')), may hold values from -6 to 6
- tet_weights: float32 [4, 524288], P(None, ('grp', 'blk')), may hold values from 0.25 to 1
- tet_cell: int32 [524288], P(('grp', 'blk')), may hold values from 0 to 32767
- tet_vertex: int32 [4, 524288], P(None, ('grp', 'blk')), may hold values from 0 to 1535
- tet_count: int32 [256, 64], P(('grp', 'blk')), may hold values from 1 to 32, as said below
Outputs:
- adjoint_field: float32 [5, 128, 65536], P(None, 'grp', 'blk')
- sensitivity: float32 [3, 393216], P(None, ('grp', 'blk'))
Inputs may be any that keep to these rules, and one draw needn't show every extreme that they name: `flow_state`: the density is 0.5 to 2, pressure 0.4 (energy - momentum squared / (2 density)) is about 0.5 to 2, each velocity component is below 1 in magnitude. A block's slots are grouped by owner: slots o * 32 to (o + 1) * 32 - 1 of a block are for owner o of its group, and the first tet_count[block, o] of them are live. In every group one owner, drawn from the seed, gets exactly 32 live tetrahedra from every block of the group. `tet_vertex`: A corner's vertex belongs to the owner of its slot's range. `tet_cell`: cell index x 32 * 32 + y * 32 + z within the block.
All inputs are finite; a program needn't handle non-finite values.
Results may differ from a plain program's by a relative error of at most 0.0003.
Values sent between devices are 32-bit elements; how exact they have to be, the bound alone decides.
A program may use at most 128 MiB of HBM per device.

v0:
```python
import jax
import jax.numpy as jnp
from jax import lax
from jax.sharding import PartitionSpec as P

SWEEPS = 2
VERT_DEV = 1536


GAMMA = 1.4


def padded(block, sides, width):
    for axis, dim in sides:
        count = lax.axis_size(axis)
        forward = [(i, i + 1) for i in range(count - 1)]
        backward = [(target, source) for source, target in forward]
        low = lax.ppermute(
            lax.slice_in_dim(block, block.shape[dim] - width, None, axis=dim), axis, forward
        )
        high = lax.ppermute(lax.slice_in_dim(block, 0, width, axis=dim), axis, backward)
        block = jnp.concatenate([low, block, high], axis=dim)
    return block


def flow_split(state):
    density = state[0]
    velocity = state[1:4] / density
    speed_sq = jnp.sum(velocity * velocity, axis=0)
    pressure = (GAMMA - 1.0) * (state[4] - 0.5 * density * speed_sq)
    return (velocity, speed_sq, pressure)


def jacobians(state):
    density = state[0]
    velocity, speed_sq, pressure = flow_split(state)
    enthalpy = (state[4] + pressure) / density
    reach = jnp.sqrt(speed_sq) + jnp.sqrt(GAMMA * pressure / density)
    half_sq = 0.5 * (GAMMA - 1.0) * speed_sq
    tables = []
    for axis_id in range(3):
        normal_vel = velocity[axis_id]
        matrix = [[1.0 if column == axis_id + 1 else 0.0 for column in range(5)]]
        for first in range(3):
            n_first = 1.0 if first == axis_id else 0.0
            line = [half_sq * n_first - velocity[first] * normal_vel]
            for second in range(3):
                n_second = 1.0 if second == axis_id else 0.0
                entry = velocity[first] * n_second - (GAMMA - 1.0) * n_first * velocity[second]
                if first == second:
                    entry = entry + normal_vel
                line.append(entry)
            line.append((GAMMA - 1.0) * n_first)
            matrix.append(line)
        energy_line = [normal_vel * (half_sq - enthalpy)]
        for second in range(3):
            n_second = 1.0 if second == axis_id else 0.0
            energy_line.append(enthalpy * n_second - (GAMMA - 1.0) * normal_vel * velocity[second])
        energy_line.append(GAMMA * normal_vel)
        matrix.append(energy_line)
        tables.append(matrix)
    return (reach, tables)


def apply_transpose(matrix, adjoint):
    result = []
    for column in range(5):
        total = matrix[0][column] * adjoint[0]
        for line in range(1, 5):
            total = total + matrix[line][column] * adjoint[line]
        result.append(total)
    return jnp.stack(result)


def relax_cells(reach, tables, faces, pseudo, rhs, neighbours):
    total = rhs
    weight = pseudo
    for direction in range(6):
        axis_id = direction // 2
        sign_value = 1.0 if direction % 2 == 0 else -1.0
        nearby = neighbours[direction]
        face = faces[direction].astype(jnp.float32)
        total = total + 0.5 * face * (
            sign_value * apply_transpose(tables[axis_id], nearby) + reach * nearby
        )
        weight = weight + 0.5 * reach * face
    return total / weight


def cross_product(left, right):
    return jnp.stack(
        [
            left[1] * right[2] - left[2] * right[1],
            left[2] * right[0] - left[0] * right[2],
            left[0] * right[1] - left[1] * right[0],
        ]
    )


def tet_terms(adj_tet, state_tet, coords, weights, live):
    velocity, speed_sq, pressure = flow_split(state_tet)
    volume_weight = pressure * adj_tet[4]
    face_weight = pressure * adj_tet[1:4]
    corner = [coords[k] for k in range(4)]
    edge_one = corner[1] - corner[0]
    edge_two = corner[2] - corner[0]
    edge_three = corner[3] - corner[0]
    grad_one = cross_product(edge_two, edge_three) / 6.0
    grad_two = cross_product(edge_three, edge_one) / 6.0
    grad_three = cross_product(edge_one, edge_two) / 6.0
    grad_zero = -(grad_one + grad_two + grad_three)
    side_one = corner[2] - corner[1]
    side_two = corner[3] - corner[1]
    face_two = 0.5 * cross_product(side_two, face_weight)
    face_three = 0.5 * cross_product(face_weight, side_one)
    face_one = -(face_two + face_three)
    terms = jnp.stack(
        [
            volume_weight * grad_zero,
            volume_weight * grad_one + face_one,
            volume_weight * grad_two + face_two,
            volume_weight * grad_three + face_three,
        ]
    )
    return terms * (weights * live)[:, None, :]


def local(
    adjoint_init,
    adjoint_rhs,
    flow_state,
    face_weights,
    pseudo_time,
    tet_coords,
    tet_weights,
    tet_cell,
    tet_vertex,
    tet_count,
):
    edge = adjoint_init.shape[1]
    span = adjoint_init.shape[2]
    owners = lax.axis_size("blk")
    tet_total = tet_cell.shape[0]
    capacity = tet_total // owners
    vertices = VERT_DEV
    column_pos = jnp.arange(span, dtype=jnp.int32) % edge
    keep_upper = (column_pos != edge - 1).astype(jnp.float32)
    keep_lower = (column_pos != 0).astype(jnp.float32)
    zero_single = jnp.zeros((5, edge, 1), jnp.float32)
    reach, tables = jacobians(flow_state)
    adjoint = adjoint_init
    for sweep_index in range(SWEEPS):
        along_x = padded(adjoint, (("grp", 1),), 1)
        along_y = padded(adjoint, (("blk", 2),), edge)
        neighbours = [
            along_x[:, 2:],
            along_x[:, :-2],
            along_y[:, :, 2 * edge :],
            along_y[:, :, : -2 * edge],
            jnp.concatenate([adjoint[:, :, 1:], zero_single], 2) * keep_upper,
            jnp.concatenate([zero_single, adjoint[:, :, :-1]], 2) * keep_lower,
        ]
        adjoint = relax_cells(reach, tables, face_weights, pseudo_time, adjoint_rhs, neighbours)
    slot = jnp.arange(tet_total, dtype=jnp.int32)
    owner_slot = slot // capacity
    slot_counts = jnp.broadcast_to(tet_count[0][:, None], (owners, capacity)).reshape(-1)
    live = (slot % capacity < slot_counts).astype(jnp.float32)
    adj_tet = jnp.take(adjoint.reshape(5, -1), tet_cell, axis=1)
    state_tet = jnp.take(flow_state.reshape(5, -1), tet_cell, axis=1)
    terms = tet_terms(adj_tet, state_tet, tet_coords, tet_weights, live)
    target = (owner_slot[None, :] * vertices + tet_vertex).reshape(-1)
    data = jnp.transpose(terms, (1, 0, 2)).reshape(3, -1)
    inside = (target >= 0) & (target < 1 * lax.axis_size("blk") * vertices)
    clipped = jnp.where(inside, target, 0)
    masked = jnp.where(inside[None, :], data, 0.0)
    summed = jax.vmap(
        lambda values: jax.ops.segment_sum(
            values, clipped, num_segments=1 * lax.axis_size("blk") * vertices
        )
    )(masked)
    sums = lax.psum_scatter(
        jnp.transpose(summed.reshape(3, 1 * lax.axis_size("blk"), vertices), (1, 0, 2)),
        "blk",
        scatter_dimension=0,
        tiled=True,
    )[0]
    return (adjoint, sums)


def solution(mesh):
    return jax.shard_map(
        local,
        mesh=mesh,
        in_specs=(
            P(None, "grp", "blk"),
            P(None, "grp", "blk"),
            P(None, "grp", "blk"),
            P(None, "grp", "blk"),
            P("grp", "blk"),
            P(None, None, ("grp", "blk")),
            P(None, ("grp", "blk")),
            P(("grp", "blk")),
            P(None, ("grp", "blk")),
            P(("grp", "blk"), None),
        ),
        out_specs=(P(None, "grp", "blk"), P(None, ("grp", "blk"))),
        check_vma=False,
    )
```

profile of v0, /device:TPU:1, one launch (start us, length us, event | category | flops | bytes accessed | tf_op | source)
XLA Modules:
  0.0 429.3 jit_solution(6481203155814915588)
XLA Ops:
  7.2 1.7 fusion.163
  8.9 4.0 collective-permute-start.1
  12.9 1.7 fusion.164
  14.6 3.9 collective-permute-start.3
  18.5 1.9 collective-permute-start.2
  20.5 1.3 collective-permute-start
  21.8 1.6 fusion.162
  24.1 1.3 compare_and_fusion
  25.4 1.2 fusion.165
  29.2 0.8 and_bitcast_fusion
  30.8 0.9 slice_bitcast_fusion
  31.7 1.1 multiply_reduce_fusion
  32.8 2.0 fusion.41
  36.3 0.9 pad_multiply_fusion.3
  37.5 2.0 fusion.48
  40.3 1.2 constant_dynamic-update-slice_fusion
  41.4 10.0 %copy.78 = f32[5,32,1024]{0,2,1:T(8,128)} copy(f32[5,32,1024]{2,1,0:T(8,128)} %param.14) | data formatting | bytes 1310720 | tf_op args[2]
  51.5 13.4 %gather_fusion = f32[2048,5]{1,0:T(8,128)} fusion(f32[5,32768]{0,1:T(8,128)} %bitcast.203, s32[2048]{0:T(1024)S(1)} %fusion.117), kind=kCustom, calls=%fused_computation.clone | custom fusion | bytes 90112 | tf_op jit(solution)/shard_map/jit(_take)/gather | solution.py:169
  64.9 2.2 copy.79
  68.3 2.1 add_dynamic-update-slice_fusion.54
  70.4 0.9 constant_dynamic-update-slice_fusion.1
  71.3 2.1 add_dynamic-update-slice_fusion.44
  73.5 2.4 add_dynamic-update-slice_fusion.39
  75.9 0.9 dynamic-update-slice.63
  77.0 1.6 add_dynamic-update-slice_fusion.34
  78.7 2.3 add_dynamic-update-slice_fusion.38
  81.0 2.0 add_dynamic-update-slice_fusion.37
  83.2 2.0 add_dynamic-update-slice_fusion.31
  85.2 0.9 add_dynamic-update-slice_fusion.48
  86.1 2.2 add_dynamic-update-slice_fusion.36
  88.3 2.1 add_dynamic-update-slice_fusion.52
  90.5 0.9 add_dynamic-update-slice_fusion.51
  91.3 0.8 add_dynamic-update-slice_fusion.50
  92.9 0.9 add_dynamic-update-slice_fusion.46
  94.0 0.9 add_dynamic-update-slice_fusion.55
  95.1 3.0 fusion.27
  98.5 1.9 collective-permute-start.6
  100.4 3.6 collective-permute-start.7
  104.0 1.3 collective-permute-start.4
  105.3 5.1 %collective-permute-start.5 = (f32[5,1,1024]{2,1,0:T(1,128)S(1)}, f32[5,1,1024]{2,1,0:T(1,128)S(1)}, u32[]{:S(2)}, u32[]{:S(2)}) collective-permute-start(f32[5,1,1024]{2,1,0:T(1,128)S(1)} %get-tuple-element.88), channel_id=1, source_target_pairs={{0,64},{64,128},{128,192},{1,65},{65,129},{129,193},{2,66},{66,130... | collective-permute-start | bytes 61448 | tf_op jit(solution)/shard_map/ppermute | solution.py:18
  113.7 1.1 fusion.8
  114.8 8.9 %copy.80 = f32[5,32,1024]{0,2,1:T(8,128)} copy(f32[5,32,1024]{2,1,0:T(8,128)S(1)} %fusion.8) | data formatting | bytes 1310720 | tf_op jit(solution)/shard_map/div | solution.py:87
  123.8 11.2 %gather_fusion.1 = f32[2048,5]{1,0:T(8,128)S(1)} fusion(f32[5,32768]{0,1:T(8,128)} %bitcast.202, s32[2048]{0:T(1024)S(1)} %copy-done.45), kind=kCustom, calls=%fused_computation.1.clone | custom fusion | bytes 90112 | tf_op jit(solution)/shard_map/jit(_take)/gather | solution.py:168
  136.1 2.6 copy.86
  138.7 64.1 %scatter_custom_fusion = f32[3,98304]{0,1:T(8,128)} fusion(s32[8192]{0:T(1024)} %bitcast.210, f32[8192,3]{1,0:T(8,128)} %copy.86, f32[]{:T(128)} %constant.69.clone.1), kind=kCustom, calls=%fused_computation.3 | custom fusion | flops 24576 | bytes 1180160 | tf_op jit(solution)/shard_map/vmap()/scatter-add | solution.py:177
  202.8 26.8 %copy.87 = f32[3,64,1536]{2,0,1:T(4,128)} copy(f32[3,64,1536]{0,2,1:T(8,128)} %bitcast.201) | data formatting | bytes 2359296 | tf_op jit(solution)/shard_map/reshape | solution.py:182
  230.2 190.2 %all-reduce.7.cloned.1.call-done = f32[64,3,1536]{2,1,0:T(4,128)} async-done(((f32[64,3,1536]{2,1,0:T(4,128)}), f32[64,3,1536]{2,1,0:T(4,128)}) %all-reduce.7.cloned.1.call-update) | async-done | bytes 1179664
  420.4 2.0 dynamic-slice_bitcast_fusion
  (191 shorter events, 14.1 us)
Async XLA Ops:
  7.2 61.1 %copy-start = (f32[5,32,1024]{2,1,0:T(8,128)S(1)}, f32[5,32,1024]{2,1,0:T(8,128)}, u32[]{:S(2)}) copy-start(f32[5,32,1024]{2,1,0:T(8,128)} %param.12) | copy-start | bytes 1966084
  7.2 413.2 %all-reduce.7.cloned.1.call-start = ((), (), s32[]{:S(2)}) async-start(), calls=%async_computation | async-start | bytes 3145728
  8.9 58.7 %collective-permute-start.1 = (f32[5,1,1024]{2,1,0:T(1,128)S(1)}, f32[5,1,1024]{2,1,0:T(1,128)S(1)}, u32[]{:S(2)}, u32[]{:S(2)}) collective-permute-start(f32[5,1,1024]{2,1,0:T(1,128)S(1)} %get-tuple-element.94), channel_id=1, source_target_pairs={{0,64},{64,128},{128,192},{1,65},{65,129},{129,193},{2,66},{66,130... | collective-permute-start | bytes 61448 | tf_op jit(solution)/shard_map/ppermute | solution.py:18
  14.6 56.8 %collective-permute-start.3 = (f32[5,32,32]{2,1,0:T(8,128)}, f32[5,32,32]{2,1,0:T(8,128)}, u32[]{:S(2)}, u32[]{:S(2)}) collective-permute-start(f32[5,32,32]{2,1,0:T(8,128)} %get-tuple-element.98), channel_id=1, source_target_pairs={{0,1},{1,2},{2,3},{3,4},{4,5},{5,6},{6,7},{7,8},{8,9},{9,10},{10,1... | collective-permute-start | bytes 61448 | tf_op jit(solution)/shard_map/ppermute | solution.py:18
  18.5 51.9 %collective-permute-start.2 = (f32[5,32,32]{2,1,0:T(8,128)}, f32[5,32,32]{2,1,0:T(8,128)}, u32[]{:S(2)}, u32[]{:S(2)}) collective-permute-start(f32[5,32,32]{2,1,0:T(8,128)} %get-tuple-element.97), channel_id=1, source_target_pairs={{1,0},{2,1},{3,2},{4,3},{5,4},{6,5},{7,6},{8,7},{9,8},{10,9},{11,1... | collective-permute-start | bytes 61448 | tf_op jit(solution)/shard_map/ppermute | solution.py:21
  20.5 55.4 %collective-permute-start = (f32[5,1,1024]{2,1,0:T(1,128)}, f32[5,1,1024]{2,1,0:T(1,128)}, u32[]{:S(2)}, u32[]{:S(2)}) collective-permute-start(f32[5,1,1024]{2,1,0:T(1,128)} %get-tuple-element.93), channel_id=1, source_target_pairs={{64,0},{128,64},{192,128},{65,1},{129,65},{193,129},{66,2},{130,66... | collective-permute-start | bytes 61448 | tf_op jit(solution)/shard_map/ppermute | solution.py:21
  24.1 43.5 %copy-start.44 = (s32[2048]{0:T(1024)}, s32[2048]{0:T(1024)S(1)}, u32[]{:S(2)}) copy-start(s32[2048]{0:T(1024)S(1)} %fusion.117) | copy-start | bytes 24580
  32.8 34.9 %copy-start.20 = (f32[32,1024]{1,0:T(8,128)}, f32[32,1024]{1,0:T(8,128)S(1)}, u32[]{:S(2)}) copy-start(f32[32,1024]{1,0:T(8,128)S(1)} %get-tuple-element.82) | copy-start | bytes 393220
  76.9 18.1 %copy-start.3 = (f32[5,32,1023]{2,1,0:T(8,128)S(1)}, f32[5,32,1023]{2,1,0:T(8,128)}, u32[]{:S(2)}) copy-start(f32[5,32,1023]{2,1,0:T(8,128)} %copy-done.2) | copy-start | bytes 1964164
  76.9 18.0 %copy-start.5 = (f32[5,32,1023]{2,1,0:T(8,128)S(1)}, f32[5,32,1023]{2,1,0:T(8,128)}, u32[]{:S(2)}) copy-start(f32[5,32,1023]{2,1,0:T(8,128)} %copy-done.4) | copy-start | bytes 1964164
  76.9 18.0 %copy-start.21 = (f32[5,32,1024]{2,1,0:T(8,128)S(1)}, f32[5,32,1024]{2,1,0:T(8,128)}, u32[]{:S(2)}) copy-start(f32[5,32,1024]{2,1,0:T(8,128)} %param.13) | copy-start | bytes 1966084
  76.9 18.0 %copy-start.29 = (f32[32,1024]{1,0:T(8,128)S(1)}, f32[32,1024]{1,0:T(8,128)}, u32[]{:S(2)}) copy-start(f32[32,1024]{1,0:T(8,128)} %get-tuple-element.141) | copy-start | bytes 393220
  76.9 18.0 %copy-start.30 = (f32[32,1024]{1,0:T(8,128)S(1)}, f32[32,1024]{1,0:T(8,128)}, u32[]{:S(2)}) copy-start(f32[32,1024]{1,0:T(8,128)} %get-tuple-element.142) | copy-start | bytes 393220
  76.9 18.0 %copy-start.31 = (f32[32,1024]{1,0:T(8,128)S(1)}, f32[32,1024]{1,0:T(8,128)}, u32[]{:S(2)}) copy-start(f32[32,1024]{1,0:T(8,128)} %get-tuple-element.143) | copy-start | bytes 393220
  76.9 18.0 %copy-start.32 = (f32[32,1024]{1,0:T(8,128)S(1)}, f32[32,1024]{1,0:T(8,128)}, u32[]{:S(2)}) copy-start(f32[32,1024]{1,0:T(8,128)} %get-tuple-element.144) | copy-start | bytes 393220
  77.0 18.0 %copy-start.33 = (f32[32,1024]{1,0:T(8,128)S(1)}, f32[32,1024]{1,0:T(8,128)}, u32[]{:S(2)}) copy-start(f32[32,1024]{1,0:T(8,128)} %get-tuple-element.145) | copy-start | bytes 393220
  77.0 18.0 %copy-start.34 = (f32[32,1024]{1,0:T(8,128)S(1)}, f32[32,1024]{1,0:T(8,128)}, u32[]{:S(2)}) copy-start(f32[32,1024]{1,0:T(8,128)} %get-tuple-element.146) | copy-start | bytes 393220
  77.0 18.0 %copy-start.35 = (f32[32,1024]{1,0:T(8,128)S(1)}, f32[32,1024]{1,0:T(8,128)}, u32[]{:S(2)}) copy-start(f32[32,1024]{1,0:T(8,128)} %get-tuple-element.84) | copy-start | bytes 393220
  77.0 18.0 %copy-start.36 = (f32[32,1024]{1,0:T(8,128)S(1)}, f32[32,1024]{1,0:T(8,128)}, u32[]{:S(2)}) copy-start(f32[32,1024]{1,0:T(8,128)} %fusion.48) | copy-start | bytes 393220
  77.0 18.0 %copy-start.43 = (f32[5,1,1024]{2,1,0:T(1,128)S(1)}, f32[5,1,1024]{2,1,0:T(1,128)}, u32[]{:S(2)}) copy-start(f32[5,1,1024]{2,1,0:T(1,128)} %copy-done.42) | copy-start | bytes 61444
  77.0 18.0 %copy-start.53 = (f32[1024]{0:T(1024)S(1)}, f32[1024]{0:T(1024)}, u32[]{:S(2)}) copy-start(f32[1024]{0:T(1024)} %copy-done.52) | copy-start | bytes 12292
  77.0 18.0 %copy-start.55 = (f32[1024]{0:T(1024)S(1)}, f32[1024]{0:T(1024)}, u32[]{:S(2)}) copy-start(f32[1024]{0:T(1024)} %copy-done.54) | copy-start | bytes 12292
  85.2 25.5 %copy-start.7 = (f32[1,32,1024]{2,1,0:T(8,128)S(1)}, f32[1,32,1024]{2,1,0:T(8,128)}, u32[]{:S(2)}) copy-start(f32[1,32,1024]{2,1,0:T(8,128)} %copy-done.6) | copy-start | bytes 393220
  85.2 25.6 %copy-start.9 = (f32[1,32,1024]{2,1,0:T(8,128)S(1)}, f32[1,32,1024]{2,1,0:T(8,128)}, u32[]{:S(2)}) copy-start(f32[1,32,1024]{2,1,0:T(8,128)} %copy-done.8) | copy-start | bytes 393220
  85.2 25.6 %copy-start.37 = (f32[1,32,1024]{2,1,0:T(8,128)S(1)}, f32[1,32,1024]{2,1,0:T(8,128)}, u32[]{:S(2)}) copy-start(f32[1,32,1024]{2,1,0:T(8,128)} %get-tuple-element.80) | copy-start | bytes 393220
  85.2 25.6 %copy-start.38 = (f32[1,32,1024]{2,1,0:T(8,128)S(1)}, f32[1,32,1024]{2,1,0:T(8,128)}, u32[]{:S(2)}) copy-start(f32[1,32,1024]{2,1,0:T(8,128)} %get-tuple-element.81) | copy-start | bytes 393220
  91.3 20.0 %copy-start.24 = (f32[1,32,1024]{2,1,0:T(8,128)S(1)}, f32[1,32,1024]{2,1,0:T(8,128)}, u32[]{:S(2)}) copy-start(f32[1,32,1024]{2,1,0:T(8,128)} %copy-done.23) | copy-start | bytes 393220
  91.3 20.0 %copy-start.26 = (f32[1,32,1024]{2,1,0:T(8,128)S(1)}, f32[1,32,1024]{2,1,0:T(8,128)}, u32[]{:S(2)}) copy-start(f32[1,32,1024]{2,1,0:T(8,128)} %copy-done.25) | copy-start | bytes 393220
  98.5 12.9 %collective-permute-start.6 = (f32[5,32,32]{2,1,0:T(8,128)S(1)}, f32[5,32,32]{2,1,0:T(8,128)S(1)}, u32[]{:S(2)}, u32[]{:S(2)}) collective-permute-start(f32[5,32,32]{2,1,0:T(8,128)S(1)} %get-tuple-element.89), channel_id=1, source_target_pairs={{1,0},{2,1},{3,2},{4,3},{5,4},{6,5},{7,6},{8,7},{9,8},{10,9},{11,1... | collective-permute-start | bytes 61448 | tf_op jit(solution)/shard_map/ppermute | solution.py:21
  100.4 11.3 %collective-permute-start.7 = (f32[5,32,32]{2,1,0:T(8,128)S(1)}, f32[5,32,32]{2,1,0:T(8,128)S(1)}, u32[]{:S(2)}, u32[]{:S(2)}) collective-permute-start(f32[5,32,32]{2,1,0:T(8,128)S(1)} %get-tuple-element.90), channel_id=1, source_target_pairs={{0,1},{1,2},{2,3},{3,4},{4,5},{5,6},{6,7},{7,8},{8,9},{9,10},{10,1... | collective-permute-start | bytes 61448 | tf_op jit(solution)/shard_map/ppermute | solution.py:18
  104.0 8.3 %collective-permute-start.4 = (f32[5,1,1024]{2,1,0:T(1,128)S(1)}, f32[5,1,1024]{2,1,0:T(1,128)S(1)}, u32[]{:S(2)}, u32[]{:S(2)}) collective-permute-start(f32[5,1,1024]{2,1,0:T(1,128)S(1)} %get-tuple-element.87), channel_id=1, source_target_pairs={{64,0},{128,64},{192,128},{65,1},{129,65},{193,129},{66,2},{130,66... | collective-permute-start | bytes 61448 | tf_op jit(solution)/shard_map/ppermute | solution.py:21
  105.3 7.3 %collective-permute-start.5 = (f32[5,1,1024]{2,1,0:T(1,128)S(1)}, f32[5,1,1024]{2,1,0:T(1,128)S(1)}, u32[]{:S(2)}, u32[]{:S(2)}) collective-permute-start(f32[5,1,1024]{2,1,0:T(1,128)S(1)} %get-tuple-element.88), channel_id=1, source_target_pairs={{0,64},{64,128},{128,192},{1,65},{65,129},{129,193},{2,66},{66,130... | collective-permute-start | bytes 61448 | tf_op jit(solution)/shard_map/ppermute | solution.py:18
  113.1 22.2 %copy-start.39 = (f32[2048,5]{0,1:T(8,128)S(1)}, f32[2048,5]{0,1:T(8,128)}, u32[]{:S(2)}) copy-start(f32[2048,5]{0,1:T(8,128)} %copy.79) | copy-start | bytes 122884
  113.1 22.2 %copy-start.60 = (pred[2048]{0:T(1024)(128)(4,1)S(1)}, pred[2048]{0:T(1024)(128)(4,1)}, u32[]{:S(2)}) copy-start(pred[2048]{0:T(1024)(128)(4,1)} %compare_and_fusion) | copy-start | bytes 6148
  113.2 22.3 %copy-start.41 = (f32[1,3,2048]{2,1,0:T(4,128)S(1)}, f32[1,3,2048]{2,1,0:T(4,128)}, u32[]{:S(2)}) copy-start(f32[1,3,2048]{2,1,0:T(4,128)} %get-tuple-element.179) | copy-start | bytes 73732
  113.2 22.4 %copy-start.40 = (f32[1,3,2048]{2,1,0:T(4,128)S(1)}, f32[1,3,2048]{2,1,0:T(4,128)}, u32[]{:S(2)}) copy-start(f32[1,3,2048]{2,1,0:T(4,128)} %get-tuple-element.183) | copy-start | bytes 73732
  113.2 22.5 %copy-start.46 = (f32[1,1,2048]{2,1,0:T(1,128)S(1)}, f32[1,1,2048]{2,1,0:T(1,128)}, u32[]{:S(2)}) copy-start(f32[1,1,2048]{2,1,0:T(1,128)} %get-tuple-element.160) | copy-start | bytes 24580
  113.2 22.5 %copy-start.47 = (f32[1,1,2048]{2,1,0:T(1,128)S(1)}, f32[1,1,2048]{2,1,0:T(1,128)}, u32[]{:S(2)}) copy-start(f32[1,1,2048]{2,1,0:T(1,128)} %get-tuple-element.161) | copy-start | bytes 24580
  113.2 22.5 %copy-start.48 = (f32[1,1,2048]{2,1,0:T(1,128)S(1)}, f32[1,1,2048]{2,1,0:T(1,128)}, u32[]{:S(2)}) copy-start(f32[1,1,2048]{2,1,0:T(1,128)} %get-tuple-element.162) | copy-start | bytes 24580
  113.2 22.5 %copy-start.49 = (f32[1,1,2048]{2,1,0:T(1,128)S(1)}, f32[1,1,2048]{2,1,0:T(1,128)}, u32[]{:S(2)}) copy-start(f32[1,1,2048]{2,1,0:T(1,128)} %get-tuple-element.166) | copy-start | bytes 24580
  113.2 22.5 %copy-start.50 = (f32[1,1,2048]{2,1,0:T(1,128)S(1)}, f32[1,1,2048]{2,1,0:T(1,128)}, u32[]{:S(2)}) copy-start(f32[1,1,2048]{2,1,0:T(1,128)} %get-tuple-element.167) | copy-start | bytes 24580
  113.2 22.5 %copy-start.51 = (f32[1,1,2048]{2,1,0:T(1,128)S(1)}, f32[1,1,2048]{2,1,0:T(1,128)}, u32[]{:S(2)}) copy-start(f32[1,1,2048]{2,1,0:T(1,128)} %get-tuple-element.168) | copy-start | bytes 24580
  113.2 22.6 %copy-start.56 = (f32[1,1,2048]{2,1,0:T(1,128)S(1)}, f32[1,1,2048]{2,1,0:T(1,128)}, u32[]{:S(2)}) copy-start(f32[1,1,2048]{2,1,0:T(1,128)} %get-tuple-element.172) | copy-start | bytes 24580
  113.2 22.6 %copy-start.57 = (f32[1,1,2048]{2,1,0:T(1,128)S(1)}, f32[1,1,2048]{2,1,0:T(1,128)}, u32[]{:S(2)}) copy-start(f32[1,1,2048]{2,1,0:T(1,128)} %get-tuple-element.173) | copy-start | bytes 24580
  113.3 22.6 %copy-start.58 = (f32[1,1,2048]{2,1,0:T(1,128)S(1)}, f32[1,1,2048]{2,1,0:T(1,128)}, u32[]{:S(2)}) copy-start(f32[1,1,2048]{2,1,0:T(1,128)} %get-tuple-element.174) | copy-start | bytes 24580
  113.4 22.6 %copy-start.59 = (pred[1,16,4,128]{3,1,2,0:T(8,128)(4,1)S(1)}, pred[1,16,4,128]{3,1,2,0:T(8,128)(4,1)}, u32[]{:S(2)}) copy-start(pred[1,16,4,128]{3,1,2,0:T(8,128)(4,1)} %copy.93) | copy-start | bytes 24580
  114.8 87.9 %copy-start.22 = (f32[5,32,1024]{2,1,0:T(8,128)}, f32[5,32,1024]{2,1,0:T(8,128)S(1)}, u32[]{:S(2)}) copy-start(f32[5,32,1024]{2,1,0:T(8,128)S(1)} %fusion.8) | copy-start | bytes 1966084
  202.8 26.8 %copy-start.61 = (u32[256]{0:T(256)S(1)}, u32[256]{0:T(256)}, u32[]{:S(2)}) copy-start(u32[256]{0:T(256)} %constant.95) | copy-start | bytes 3076
  (23 other events, 274.3 us)
Sparse Core Ops, SparseCore 0:
  229.7 190.6 all-reduce.6
where the time goes:
time: 432 us; the launch traced here: 429 us
  waiting for transfers between devices  190 us (44%)
  other arithmetic  110 us (25%)
  local copies, waits for them, and re-layouts  90.9 us (21%)
  starting transfers between devices  23.2 us (5%)
  between operations  15.2 us (4%)
    unnamed x2, waiting for transfers between devices  190 us
    scatter-add x1, other arithmetic, local(): jax.ops.segment_sum(values, clipped, num_segments=1 * lax.axis_size('blk'...  64.1 us
    reshape x1, local copies, waits for them, and re-layouts, local(): summed.reshape(3, 1 * lax.axis_size('blk'), vertices)  26.8 us
    unnamed x32, other arithmetic  25.7 us
    ppermute x4, starting transfers between devices, padded(): lax.ppermute(lax.slice_in_dim(block, block.shape[dim] - width, None, axis...  16.7 us
    gather x2, local copies, waits for them, and re-layouts, local(): state_tet = jnp.take(flow_state.reshape(5, -1), tet_cell, axis=1)  15.5 us
    unnamed x129, local copies, waits for them, and re-layouts  13.4 us
    gather x2, local copies, waits for them, and re-layouts, local(): adj_tet = jnp.take(adjoint.reshape(5, -1), tet_cell, axis=1)  11.6 us
  transfers between devices with their start and end apart: 9, of which 1 were waited for; matrix products, arithmetic and copies ran while one was open for 13% of the time, Pallas kernels for 0%

commit v1 on v0

v1 whole, which is shorter than its diff:
```python
import functools

import jax
import jax.numpy as jnp
from jax import lax
from jax.experimental import pallas as pl
from jax.experimental.pallas import tpu as pltpu
from jax.sharding import PartitionSpec as P

SWEEPS = 2
VERT_DEV = 1536
CAP = 32
LANES = 128
GAMMA = 1.4
LOCAL = 8
MESH = pl.DeviceIdType.MESH
F32 = jnp.float32
BF16 = jnp.bfloat16


def lane_iota(shape):
    return lax.broadcasted_iota(jnp.int32, shape, len(shape) - 1)


def row_iota(shape):
    return lax.broadcasted_iota(jnp.int32, shape, len(shape) - 2)


def cross(a, b):
    return [
        a[1] * b[2] - a[2] * b[1],
        a[2] * b[0] - a[0] * b[2],
        a[0] * b[1] - a[1] * b[0],
    ]


def kernel(
    groups,
    blocks,
    init_hbm,
    rhs_hbm,
    flow_hbm,
    face_hbm,
    pseudo_hbm,
    coords_hbm,
    weights_hbm,
    cell_hbm,
    vertex_hbm,
    count_hbm,
    adj_out,
    sens_out,
    adj_a,
    adj_b,
    adj_c,
    rhs,
    flow,
    face,
    pseudo,
    coords,
    weights,
    cell,
    vertex,
    count,
    gface,
    scaled,
    coef,
    press,
    y_send,
    y_recv,
    table,
    onehot,
    geom,
    send,
    recv,
    left_op,
    right_op,
    load_sem,
    out_sem,
    halo_send,
    halo_recv,
    term_send,
    term_recv,
):
    group = lax.axis_index("grp")
    block = lax.axis_index("blk")
    columns = 8
    chunks = blocks // 8

    loads = [
        (flow_hbm, flow),
        (face_hbm, face),
        (pseudo_hbm, pseudo),
        (rhs_hbm, rhs),
        (cell_hbm, cell),
        (coords_hbm, coords),
        (weights_hbm, weights),
        (vertex_hbm, vertex),
        (count_hbm, count),
    ]
    for tile in range(columns):
        pltpu.make_async_copy(
            init_hbm.at[:, :, pl.ds(tile * LANES, LANES)],
            adj_a.at[:, 1 + tile, pl.ds(8, 32), :],
            load_sem.at[len(loads)],
        ).start()
    for position, (source, target) in enumerate(loads):
        pltpu.make_async_copy(source, target, load_sem.at[position]).start()

    def loaded(*wanted):
        for position, (source, target) in enumerate(loads):
            if any(target is one for one in wanted):
                pltpu.make_async_copy(source, target, load_sem.at[position]).wait()

    def inner(ref):
        return ref.at[:, pl.ds(1, columns), pl.ds(8, 32), :]

    grp_up = {"grp": lax.rem(group + 1, groups)}
    grp_down = {"grp": lax.rem(group + groups - 1, groups)}
    blk_up = {"blk": lax.rem(block + 1, blocks)}
    blk_down = {"blk": lax.rem(block + blocks - 1, blocks)}

    barrier = pltpu.get_barrier_semaphore()
    for device in (grp_up, grp_down):
        pl.semaphore_signal(barrier, inc=1, device_id=device, device_id_type=MESH)

    def greet(step, carry):
        pl.semaphore_signal(
            barrier,
            inc=1,
            device_id={"blk": lax.rem(block + step, blocks)},
            device_id_type=MESH,
        )
        return carry

    lax.fori_loop(1, blocks, greet, 0)

    tile_lane = lane_iota((8, LANES))
    lane_block = tile_lane // CAP

    def halo_copies(adj, sweep):
        span = pl.ds(1, columns)
        parts = [
            (adj.at[:, span, pl.ds(39, 1), :], adj.at[:, span, pl.ds(7, 1), :], grp_up),
            (adj.at[:, span, pl.ds(8, 1), :], adj.at[:, span, pl.ds(40, 1), :], grp_down),
            (y_send.at[sweep, 0], y_recv.at[sweep, 0], blk_up),
            (y_send.at[sweep, 1], y_recv.at[sweep, 1], blk_down),
        ]
        return [
            pltpu.make_async_remote_copy(
                src_ref=source,
                dst_ref=target,
                send_sem=halo_send.at[sweep, position],
                recv_sem=halo_recv.at[sweep, position],
                device_id=device,
                device_id_type=MESH,
            )
            for position, (source, target, device) in enumerate(parts)
        ]

    def pack(adj, sweep):
        for field in range(5):
            for side, tile, home in ((0, columns, 3), (1, 1, 0)):
                total = None
                for part in range(4):
                    value = adj[field, tile, pl.ds(8 + 8 * part, 8), :]
                    turn = (part - home) % 4 * CAP
                    if turn:
                        value = pltpu.roll(value, turn, 1)
                    total = value if total is None else jnp.where(lane_block == part, value, total)
                y_send[sweep, side, field] = total

    def unpack(adj, sweep):
        for field in range(5):
            for side, tile, home in ((0, 0, 3), (1, columns + 1, 0)):
                value = y_recv[sweep, side, field]
                for part in range(4):
                    turn = (home - part) % 4 * CAP
                    adj[field, tile, pl.ds(8 + 8 * part, 8), :] = (
                        pltpu.roll(value, turn, 1) if turn else value
                    )

    def sweep_tile(source, store, tile, part):
        rows = pl.ds(8 * part, 8)
        here = pl.ds(8 * part + 8, 8)
        center = [source[f, tile + 1, here, :] for f in range(5)]
        upper = [source[f, tile + 2, here, :] for f in range(5)]
        lower = [source[f, tile, here, :] for f in range(5)]
        pairs = [
            (
                [source[f, tile + 1, pl.ds(8 * part + 9, 8), :] for f in range(5)],
                [source[f, tile + 1, pl.ds(8 * part + 7, 8), :] for f in range(5)],
            ),
            (
                [
                    pltpu.roll(jnp.where(tile_lane >= CAP, center[f], upper[f]), LANES - CAP, 1)
                    for f in range(5)
                ],
                [
                    pltpu.roll(jnp.where(tile_lane < LANES - CAP, center[f], lower[f]), CAP, 1)
                    for f in range(5)
                ],
            ),
            (
                [pltpu.roll(center[f], LANES - 1, 1) for f in range(5)],
                [pltpu.roll(center[f], 1, 1) for f in range(5)],
            ),
        ]
        velocity = [coef[k, tile, rows, :] for k in range(3)]
        half_sq = coef[3, tile, rows, :]
        enthalpy = coef[4, tile, rows, :]
        reach = coef[5, tile, rows, :]
        sums = None
        moved = None
        flux = None
        first = []
        turned = None
        for axis, (plus, minus) in enumerate(pairs):
            g_plus = gface[2 * axis, tile, rows, :]
            g_minus = gface[2 * axis + 1, tile, rows, :]
            ahead = [g_plus * value for value in plus]
            behind = [g_minus * value for value in minus]
            diff = [a - b for a, b in zip(ahead, behind)]
            both = [a + b for a, b in zip(ahead, behind)]
            sums = both if sums is None else [a + b for a, b in zip(sums, both)]
            dot = (
                velocity[0] * diff[1]
                + velocity[1] * diff[2]
                + velocity[2] * diff[3]
                + enthalpy * diff[4]
            )
            first.append(diff[0] + dot)
            speed = velocity[axis]
            part_moved = [speed * diff[k] for k in range(1, 5)]
            moved = part_moved if moved is None else [a + b for a, b in zip(moved, part_moved)]
            flux = speed * dot if flux is None else flux + speed * dot
            turned = diff[1 + axis] if turned is None else turned + diff[1 + axis]
        turned = turned + moved[3]
        scaled_turn = (GAMMA - 1.0) * turned
        result = [half_sq * turned - flux]
        for k in range(3):
            result.append(first[k] - scaled_turn * velocity[k] + moved[k])
        result.append(scaled_turn + moved[3])
        for f in range(5):
            store(f, tile, part, scaled[f, tile, rows, :] + reach * sums[f] + result[f])

    def store_b(f, tile, part, value):
        adj_b[f, tile + 1, pl.ds(8 * part + 8, 8), :] = value

    def store_c(f, tile, part, value):
        adj_c[f, pl.ds(8 * part, 8), pl.ds(pl.multiple_of(tile * LANES, LANES), LANES)] = value

    def interior(source, store):
        def body(tile, carry):
            for part in (1, 2):
                sweep_tile(source, store, tile, part)
            return carry

        lax.fori_loop(1, columns - 1, body, 0)

    def boundary(source, store):
        def body(tile, carry):
            for part in (0, 3):
                sweep_tile(source, store, tile, part)
            return carry

        lax.fori_loop(0, columns, body, 0)

        def ends(step, carry):
            for part in (1, 2):
                sweep_tile(source, store, step * (columns - 1), part)
            return carry

        lax.fori_loop(0, 2, ends, 0)

    pltpu.make_async_copy(inner(adj_a), inner(adj_a), load_sem.at[len(loads)]).wait()
    pack(adj_a, 0)
    pl.semaphore_wait(barrier, blocks + 1)
    first_halo = halo_copies(adj_a, 0)
    for copy in first_halo:
        copy.start()

    loaded(flow, face, pseudo, rhs)
    tall_row = row_iota((16, LANES))
    tall_lane = lane_iota((16, LANES))

    def coefficients(step, carry):
        tile = step // 2
        half = step % 2
        rows = pl.ds(pl.multiple_of(half * 16, 16), 16)
        lanes = pl.ds(pl.multiple_of(tile * LANES, LANES), LANES)
        density = flow[0, rows, lanes]
        inverse = 1.0 / density
        velocity = [flow[1 + k, rows, lanes] * inverse for k in range(3)]
        energy = flow[4, rows, lanes]
        speed_sq = (
            velocity[0] * velocity[0] + velocity[1] * velocity[1] + velocity[2] * velocity[2]
        )
        pressure = (GAMMA - 1.0) * (energy - 0.5 * density * speed_sq)
        enthalpy = (energy + pressure) * inverse
        reach = jnp.sqrt(speed_sq) + jnp.sqrt(GAMMA * pressure * inverse)
        for k in range(3):
            coef[k, tile, rows, :] = velocity[k]
        coef[3, tile, rows, :] = 0.5 * (GAMMA - 1.0) * speed_sq
        coef[4, tile, rows, :] = enthalpy
        coef[5, tile, rows, :] = reach
        press[tile, rows, :] = pressure
        faces = [face[d, rows, lanes].astype(F32) for d in range(6)]
        open_sum = faces[0] + faces[1] + faces[2] + faces[3] + faces[4] + faces[5]
        share = 1.0 / (pseudo[rows, lanes] + 0.5 * reach * open_sum)
        half_share = 0.5 * share
        across = tall_row + half * 16
        along = tall_lane + tile * LANES
        height = tall_lane % 32
        outside = [
            (across == 31) & (group == groups - 1),
            (across == 0) & (group == 0),
            (along >= 992) & (block == blocks - 1),
            (along < 32) & (block == 0),
            height == 31,
            height == 0,
        ]
        for d in range(6):
            gface[d, tile, rows, :] = jnp.where(outside[d], 0.0, faces[d] * half_share)
        for f in range(5):
            scaled[f, tile, rows, :] = rhs[f, rows, lanes] * share
        return carry

    lax.fori_loop(0, 2 * columns, coefficients, 0)
    interior(adj_a, store_b)
    for copy in first_halo:
        copy.wait_recv()
    unpack(adj_a, 0)
    boundary(adj_a, store_b)

    pack(adj_b, 1)
    second_halo = halo_copies(adj_b, 1)
    for copy in second_halo:
        copy.start()
    interior(adj_b, store_c)

    loaded(cell, coords, weights, vertex, count)

    def pick_cells(chunk, carry):
        lanes = pl.ds(pl.multiple_of(chunk * 256, 256), 256)
        place = jnp.bitwise_and(cell[:, lanes], 1023)
        for band in range(8):
            rows = band * 128 + row_iota((128, 256))
            onehot[pl.ds(band * 128, 128), lanes] = jnp.where(rows == place, 1.0, 0.0).astype(BF16)
        return carry

    lax.fori_loop(0, chunks, pick_cells, 0)

    tile_row = row_iota((8, LANES))
    own_block = lane_block == tile_row % 4
    upper_half = tile_row < 4
    slot = tile_lane % CAP

    def spread(even, odd):
        value = jnp.where(own_block, jnp.where(upper_half, even, odd), 0.0)
        value = value + pltpu.roll(value, CAP, 1)
        return value + pltpu.roll(value, 2 * CAP, 1)

    def by_corner(values):
        total = values[3]
        for k in range(3):
            total = jnp.where(lane_block == k, values[k], total)
        return total

    def geometry(chunk, carry):
        even = pl.ds(pl.multiple_of(chunk * 256, 128), 128)
        odd = pl.ds(pl.multiple_of(chunk * 256 + 128, 128), 128)
        rows = pl.ds(pl.multiple_of(chunk * 8, 8), 8)
        corner = [
            [spread(coords[k, c : c + 1, even], coords[k, c : c + 1, odd]) for k in range(3)]
            for c in range(4)
        ]
        edge = [[corner[c][k] - corner[0][k] for k in range(3)] for c in range(1, 4)]
        grads = [
            [value / 6.0 for value in cross(edge[1], edge[2])],
            [value / 6.0 for value in cross(edge[2], edge[0])],
            [value / 6.0 for value in cross(edge[0], edge[1])],
        ]
        grad_zero = [-(grads[0][k] + grads[1][k] + grads[2][k]) for k in range(3)]
        side_two = [0.5 * (corner[3][k] - corner[1][k]) for k in range(3)]
        side_three = [-0.5 * (corner[2][k] - corner[1][k]) for k in range(3)]
        side_one = [-(side_two[k] + side_three[k]) for k in range(3)]
        weight = by_corner([spread(weights[c : c + 1, even], weights[c : c + 1, odd]) for c in range(4)])
        counts = jnp.broadcast_to(count[...], (8, blocks))
        wanted = lane_iota((8, blocks)) == chunk * 8 + row_iota((8, blocks))
        own_count = jnp.sum(jnp.where(wanted, counts, 0), axis=1, keepdims=True)
        weight = jnp.where(slot < own_count, weight, 0.0)
        for k in range(3):
            gradient = by_corner([grad_zero[k], grads[0][k], grads[1][k], grads[2][k]])
            side = by_corner([jnp.zeros_like(side_one[k]), side_one[k], side_two[k], side_three[k]])
            geom[k, rows, :] = weight * gradient
            geom[3 + k, rows, :] = weight * side
        send[3, rows, :] = by_corner(
            [
                spread(vertex[c : c + 1, even].astype(F32), vertex[c : c + 1, odd].astype(F32))
                for c in range(4)
            ]
        )
        return carry

    lax.fori_loop(0, chunks, geometry, 0)

    for copy in second_halo:
        copy.wait_recv()
    unpack(adj_b, 1)
    boundary(adj_b, store_c)
    adj_copy = pltpu.make_async_copy(adj_c, adj_out, out_sem)
    adj_copy.start()

    def fill_table(step, carry):
        tile = step // 2
        half = step % 2
        rows = pl.ds(pl.multiple_of(half * 16, 16), 16)
        lanes = pl.ds(pl.multiple_of(tile * LANES, LANES), LANES)
        pressure = press[tile, rows, :]
        for f in range(4):
            value = pressure * adj_c[1 + f, rows, lanes]
            high = value.astype(BF16)
            low = (value - high.astype(F32)).astype(BF16)
            table[pl.ds(pl.multiple_of(f * 32 + half * 16, 16), 16), lanes] = high
            table[pl.ds(pl.multiple_of(128 + f * 32 + half * 16, 16), 16), lanes] = low
        return carry

    lax.fori_loop(0, 2 * columns, fill_table, 0)

    def terms(chunk, carry):
        lanes = pl.ds(pl.multiple_of(chunk * 256, 256), 256)
        rows = pl.ds(pl.multiple_of(chunk * 8, 8), 8)
        found = jnp.dot(table[...], onehot[:, lanes], preferred_element_type=F32)
        found = found[:128] + found[128:]
        plane = jnp.right_shift(cell[:, lanes], 10)
        mine = row_iota((32, 256)) == plane
        fields = []
        for f in range(4):
            value = jnp.where(mine, found[32 * f : 32 * f + 32], 0.0)
            value = jnp.sum(value, axis=0, keepdims=True)
            fields.append(spread(value[:, :128], value[:, 128:]))
        b, a = fields[:3], fields[3]
        gradient = [geom[k, rows, :] for k in range(3)]
        side = [geom[3 + k, rows, :] for k in range(3)]
        turn = cross(side, b)
        for k in range(3):
            send[k, rows, :] = a * gradient[k] + turn[k]
        return carry

    lax.fori_loop(0, chunks, terms, 0)

    planes = blocks // LOCAL
    z, x, core = block // LOCAL, block % LOCAL // 2, block % 2

    def partner(step):
        far = step // LOCAL
        near = step % LOCAL
        return (
            lax.rem(z + far, planes) * LOCAL
            + lax.rem(x + near // 2, 4) * 2
            + lax.rem(core + near % 2, 2)
        )

    def post(step, carry):
        owner = partner(step)
        pltpu.make_async_remote_copy(
            src_ref=send.at[:, pl.ds(owner, 1), :],
            dst_ref=recv.at[:, pl.ds(step - 1, 1), :],
            send_sem=term_send,
            recv_sem=term_recv,
            device_id={"blk": owner},
            device_id_type=MESH,
        ).start()
        return carry

    lax.fori_loop(1, blocks, post, 0)
    recv[:, pl.ds(blocks - 1, 1), :] = send[:, pl.ds(block, 1), :]
    others = pltpu.make_async_remote_copy(
        src_ref=send.at[:, pl.ds(0, blocks - 1), :],
        dst_ref=recv.at[:, pl.ds(0, blocks - 1), :],
        send_sem=term_send,
        recv_sem=term_recv,
        device_id=blk_up,
        device_id_type=MESH,
    )
    others.wait_recv()

    def operands(chunk, carry):
        rows = pl.ds(pl.multiple_of(chunk * 8, 8), 8)
        vertices = recv[3, rows, :].astype(jnp.int32)
        major = jnp.right_shift(vertices, 7)
        minor = jnp.bitwise_and(vertices, 127)
        halves = []
        for k in range(3):
            value = recv[k, rows, :]
            high = value.astype(BF16).astype(F32)
            halves += [high, value - high]
        for s in range(8):
            lanes = pl.ds(pl.multiple_of(chunk * 1024 + s * LANES, LANES), LANES)
            right_op[:, lanes] = jnp.where(row_iota((128, LANES)) == minor[s : s + 1], 1.0, 0.0).astype(BF16)
            hit = row_iota((16, LANES)) == major[s : s + 1]
            for n, value in enumerate(halves):
                left_op[pl.ds(16 * n, 16), lanes] = jnp.where(hit, value[s : s + 1], 0.0).astype(BF16)
        return carry

    lax.fori_loop(0, chunks, operands, 0)
    sums = lax.dot_general(
        left_op[...], right_op[...], (((1,), (1,)), ((), ())), preferred_element_type=F32
    )
    for k in range(3):
        both = sums[32 * k : 32 * k + 16] + sums[32 * k + 16 : 32 * k + 32]
        for h in range(VERT_DEV // LANES):
            sens_out[k : k + 1, h * LANES : (h + 1) * LANES] = both[h : h + 1]

    for copy in first_halo + second_halo:
        copy.wait_send()
    others.wait_send()
    adj_copy.wait()


def local(groups, blocks, init, rhs, flow, face, pseudo, coords, weights, cell, vertex, count):
    slots = blocks * CAP
    vmem = pltpu.VMEM
    return pl.pallas_call(
        functools.partial(kernel, groups, blocks),
        out_shape=(
            jax.ShapeDtypeStruct((5, 32, 1024), F32),
            jax.ShapeDtypeStruct((3, VERT_DEV), F32),
        ),
        in_specs=[pl.BlockSpec(memory_space=pl.ANY)] * 10,
        out_specs=(
            pl.BlockSpec(memory_space=pl.ANY),
            pl.BlockSpec(memory_space=pltpu.VMEM),
        ),
        scratch_shapes=[
            vmem((5, 10, 48, LANES), F32),
            vmem((5, 10, 48, LANES), F32),
            vmem((5, 32, 1024), F32),
            vmem((5, 32, 1024), F32),
            vmem((5, 32, 1024), F32),
            vmem((6, 32, 1024), BF16),
            vmem((32, 1024), F32),
            vmem((3, 4, slots), F32),
            vmem((4, slots), F32),
            vmem((1, slots), jnp.int32),
            vmem((4, slots), jnp.int32),
            vmem((1, blocks), jnp.int32),
            vmem((6, 8, 32, LANES), F32),
            vmem((5, 8, 32, LANES), F32),
            vmem((6, 8, 32, LANES), F32),
            vmem((8, 32, LANES), F32),
            vmem((SWEEPS, 2, 5, 8, LANES), F32),
            vmem((SWEEPS, 2, 5, 8, LANES), F32),
            vmem((256, 1024), BF16),
            vmem((1024, slots), BF16),
            vmem((6, blocks, LANES), F32),
            vmem((4, blocks, LANES), F32),
            vmem((4, blocks, LANES), F32),
            vmem((96, slots * 4), BF16),
            vmem((128, slots * 4), BF16),
            pltpu.SemaphoreType.DMA((10,)),
            pltpu.SemaphoreType.DMA,
            pltpu.SemaphoreType.DMA((SWEEPS, 4)),
            pltpu.SemaphoreType.DMA((SWEEPS, 4)),
            pltpu.SemaphoreType.DMA,
            pltpu.SemaphoreType.DMA,
        ],
        compiler_params=pltpu.CompilerParams(
            collective_id=0, has_side_effects=True, vmem_limit_bytes=60 * 1024 * 1024
        ),
    )(
        init,
        rhs,
        flow,
        face,
        pseudo,
        jnp.transpose(coords, (1, 0, 2)),
        weights,
        cell.reshape(1, slots),
        vertex,
        count,
    )


def solution(mesh):
    return jax.shard_map(
        functools.partial(local, mesh.shape["grp"], mesh.shape["blk"]),
        mesh=mesh,
        in_specs=(
            P(None, "grp", "blk"),
            P(None, "grp", "blk"),
            P(None, "grp", "blk"),
            P(None, "grp", "blk"),
            P("grp", "blk"),
            P(None, None, ("grp", "blk")),
            P(None, ("grp", "blk")),
            P(("grp", "blk")),
            P(None, ("grp", "blk")),
            P(("grp", "blk"), None),
        ),
        out_specs=(P(None, "grp", "blk"), P(None, ("grp", "blk"))),
        check_vma=False,
    )
```

time: 432 us -> 39 us (0.09)
  waiting for transfers between devices: 190 us -> 0 us
  other arithmetic: 110 us -> 0 us
  local copies, waits for them, and re-layouts: 90.9 us -> 2.6 us
  Pallas kernels: 0 us -> 35.6 us
  starting transfers between devices: 23.2 us -> 0 us
  between operations: 15.2 us -> 0.65 us
    unnamed x2 -> x0, waiting for transfers between devices: 190 us -> none
    scatter-add x1 -> x0, other arithmetic: 64.1 us -> none  [local(): jax.ops.segment_sum(values, clipped, num_segments=1 * lax.axis_size('blk'...]
    pallas_call x0 -> x1, Pallas kernels: none -> 35.6 us  [local(): pl.pallas_call(functools.partial(kernel, groups, blocks), out_shape=(jax....]
    gather x4 -> x0, local copies, waits for them, and re-layouts: 27.1 us -> none  [the longest x2 15.5 us: local(): state_tet = jnp.take(flow_state.reshape(5, -1), tet_cell, axis=1)]
    reshape x2 -> x0, local copies, waits for them, and re-layouts: 26.8 us -> none  [the longest x1 26.8 us: local(): summed.reshape(3, 1 * lax.axis_size('blk'), vertices)]
    unnamed x32 -> x0, other arithmetic: 25.7 us -> none
    ppermute x8 -> x0, starting transfers between devices: 23.1 us -> none  [the longest x4 16.7 us: padded(): lax.ppermute(lax.slice_in_dim(block, block.shape[dim] - width, None, axis...]
    unnamed x129 -> x4, local copies, waits for them, and re-layouts: 13.4 us -> 2.6 us
  transfers between devices with their start and end apart: 9 -> 0, of which waited for: 1 -> 0; matrix products, arithmetic and copies ran while one was open for 13% -> 0% of each run, Pallas kernels for 0% -> 0%
where the time goes in v1:
time: 39 us; the launch traced here: 38.9 us
  Pallas kernels  35.6 us (91%)
  local copies, waits for them, and re-layouts  2.6 us (7%)
  between operations  0.65 us (2%)
    pallas_call x1, Pallas kernels, local(): pl.pallas_call(functools.partial(kernel, groups, blocks), out_shape=(jax....  35.6 us
    unnamed x4, local copies, waits for them, and re-layouts  2.6 us

profile of v1, /device:TPU:1, one launch (start us, length us, event | category | flops | bytes accessed | tf_op | source)
XLA Modules:
  0.0 38.9 jit_solution(18101159102840861441)
XLA Ops:
  0.6 35.6 %shard_map.113 = (f32[5,32,1024]{2,1,0:T(8,128)}, f32[3,1536]{1,0:T(4,128)}) custom-call(f32[5,32,1024]{2,1,0:T(8,128)} %init_hbm.1, f32[5,32,1024]{2,1,0:T(8,128)} %rhs_hbm.1, f32[5,32,1024]{2,1,0:T(8,128)} %flow_hbm.1, bf16[6,32,1024]{2,1,0:T(8,128)(2,1)} %face_hbm.1, f32[32,1024]{1,0:T(8,128)} %pseudo_hbm.1, f32[3,4,2048]{2,1,0:T(4,128)} %bitcast.2, ...), custom_call_target="tpu_custom_call" | custom-call | tf_op jit(solution)/shard_map/pallas_call | solution.py:524
  36.2 0.0 copy-start
  36.3 2.0 %copy.14 = f32[5,32,1024]{2,1,0:T(8,128)} copy(f32[5,32,1024]{2,1,0:T(8,128)} %get-tuple-element.4) | data formatting | bytes 1310720
  38.2 0.0 copy-done
  38.3 0.6 %copy.15 = f32[3,1536]{1,0:T(4,128)} copy(f32[3,1536]{1,0:T(4,128)S(1)} %copy-done) | data formatting | bytes 36864
Async XLA Ops:
  36.2 2.0 %copy-start = (f32[3,1536]{1,0:T(4,128)S(1)}, f32[3,1536]{1,0:T(4,128)}, u32[]{:S(2)}) copy-start(f32[3,1536]{1,0:T(4,128)} %get-tuple-element.5) | copy-start | bytes 55300

commit v2 on v1

--- a/solution.py
+++ b/solution.py
@@ -48,7 +48,7 @@
     vertex_hbm,
     count_hbm,
     adj_out,
-    sens_out,
+    recv,
     adj_a,
     adj_b,
     adj_c,
@@ -69,11 +69,9 @@
     y_recv,
     table,
     onehot,
+    found,
     geom,
     send,
-    recv,
-    left_op,
-    right_op,
     load_sem,
     out_sem,
     halo_send,
@@ -255,7 +253,7 @@
                 sweep_tile(source, store, tile, part)
             return carry
 
-        lax.fori_loop(1, columns - 1, body, 0)
+        lax.fori_loop(1, columns - 1, body, 0, unroll=4)
 
     def boundary(source, store):
         def body(tile, carry):
@@ -263,7 +261,7 @@
                 sweep_tile(source, store, tile, part)
             return carry
 
-        lax.fori_loop(0, columns, body, 0)
+        lax.fori_loop(0, columns, body, 0, unroll=4)
 
         def ends(step, carry):
             for part in (1, 2):
@@ -325,7 +323,7 @@
             scaled[f, tile, rows, :] = rhs[f, rows, lanes] * share
         return carry
 
-    lax.fori_loop(0, 2 * columns, coefficients, 0)
+    lax.fori_loop(0, 2 * columns, coefficients, 0, unroll=2)
     interior(adj_a, store_b)
     for copy in first_halo:
         copy.wait_recv()
@@ -402,13 +400,13 @@
         )
         return carry
 
-    lax.fori_loop(0, chunks, geometry, 0)
+    lax.fori_loop(0, chunks, geometry, 0, unroll=4)
 
     for copy in second_halo:
         copy.wait_recv()
     unpack(adj_b, 1)
     boundary(adj_b, store_c)
-    adj_copy = pltpu.make_async_copy(adj_c, adj_out, out_sem)
+    adj_copy = pltpu.make_async_copy(adj_c, adj_out, out_sem.at[0])
     adj_copy.start()
 
     def fill_table(step, carry):
@@ -427,17 +425,17 @@
 
     lax.fori_loop(0, 2 * columns, fill_table, 0)
 
+    found[...] = jnp.dot(table[...], onehot[...], preferred_element_type=F32)
+
     def terms(chunk, carry):
         lanes = pl.ds(pl.multiple_of(chunk * 256, 256), 256)
         rows = pl.ds(pl.multiple_of(chunk * 8, 8), 8)
-        found = jnp.dot(table[...], onehot[:, lanes], preferred_element_type=F32)
-        found = found[:128] + found[128:]
         plane = jnp.right_shift(cell[:, lanes], 10)
         mine = row_iota((32, 256)) == plane
         fields = []
         for f in range(4):
-            value = jnp.where(mine, found[32 * f : 32 * f + 32], 0.0)
-            value = jnp.sum(value, axis=0, keepdims=True)
+            value = found[32 * f : 32 * f + 32, lanes] + found[128 + 32 * f : 160 + 32 * f, lanes]
+            value = jnp.sum(jnp.where(mine, value, 0.0), axis=0, keepdims=True)
             fields.append(spread(value[:, :128], value[:, 128:]))
         b, a = fields[:3], fields[3]
         gradient = [geom[k, rows, :] for k in range(3)]
@@ -447,7 +445,7 @@
             send[k, rows, :] = a * gradient[k] + turn[k]
         return carry
 
-    lax.fori_loop(0, chunks, terms, 0)
+    lax.fori_loop(0, chunks, terms, 0, unroll=8)
 
     planes = blocks // LOCAL
     z, x, core = block // LOCAL, block % LOCAL // 2, block % 2
@@ -474,7 +472,10 @@
         return carry
 
     lax.fori_loop(1, blocks, post, 0)
-    recv[:, pl.ds(blocks - 1, 1), :] = send[:, pl.ds(block, 1), :]
+    own = pltpu.make_async_copy(
+        send.at[:, pl.ds(block, 1), :], recv.at[:, pl.ds(blocks - 1, 1), :], out_sem.at[1]
+    )
+    own.start()
     others = pltpu.make_async_remote_copy(
         src_ref=send.at[:, pl.ds(0, blocks - 1), :],
         dst_ref=recv.at[:, pl.ds(0, blocks - 1), :],
@@ -484,6 +485,30 @@
         device_id_type=MESH,
     )
     others.wait_recv()
+    own.wait()
+
+    for copy in first_halo + second_halo:
+        copy.wait_send()
+    others.wait_send()
+    adj_copy.wait()
+
+
+def vertex_sums(adj, recv_hbm, adj_out, sens_out, recv, held, left_op, right_op, recv_sem, in_sem, back_sem):
+    recv_copy = pltpu.make_async_copy(recv_hbm, recv, recv_sem)
+    recv_copy.start()
+    inward = [
+        pltpu.make_async_copy(adj.at[f], held.at[f], in_sem.at[f]) for f in range(5)
+    ]
+    outward = [
+        pltpu.make_async_copy(held.at[f], adj_out.at[f], back_sem.at[f]) for f in range(5)
+    ]
+    for copy in inward:
+        copy.start()
+    for arriving, leaving in zip(inward, outward):
+        arriving.wait()
+        leaving.start()
+    recv_copy.wait()
+    chunks = recv.shape[1] // 8
 
     def operands(chunk, carry):
         rows = pl.ds(pl.multiple_of(chunk * 8, 8), 8)
@@ -512,25 +537,23 @@
         for h in range(VERT_DEV // LANES):
             sens_out[k : k + 1, h * LANES : (h + 1) * LANES] = both[h : h + 1]
 
-    for copy in first_halo + second_halo:
-        copy.wait_send()
-    others.wait_send()
-    adj_copy.wait()
+    for copy in outward:
+        copy.wait()
 
 
 def local(groups, blocks, init, rhs, flow, face, pseudo, coords, weights, cell, vertex, count):
     slots = blocks * CAP
     vmem = pltpu.VMEM
-    return pl.pallas_call(
+    adjoint, received = pl.pallas_call(
         functools.partial(kernel, groups, blocks),
         out_shape=(
             jax.ShapeDtypeStruct((5, 32, 1024), F32),
-            jax.ShapeDtypeStruct((3, VERT_DEV), F32),
+            jax.ShapeDtypeStruct((4, blocks, LANES), F32),
         ),
-        in_specs=[pl.BlockSpec(memory_space=pl.ANY)] * 10,
+        in_specs=[pl.BlockSpec(memory_space=pltpu.HBM)] * 10,
         out_specs=(
             pl.BlockSpec(memory_space=pl.ANY),
-            pl.BlockSpec(memory_space=pltpu.VMEM),
+            pl.BlockSpec(memory_space=pl.ANY),
         ),
         scratch_shapes=[
             vmem((5, 10, 48, LANES), F32),
@@ -553,13 +576,11 @@
             vmem((SWEEPS, 2, 5, 8, LANES), F32),
             vmem((256, 1024), BF16),
             vmem((1024, slots), BF16),
+            vmem((256, slots), F32),
             vmem((6, blocks, LANES), F32),
             vmem((4, blocks, LANES), F32),
-            vmem((4, blocks, LANES), F32),
-            vmem((96, slots * 4), BF16),
-            vmem((128, slots * 4), BF16),
             pltpu.SemaphoreType.DMA((10,)),
-            pltpu.SemaphoreType.DMA,
+            pltpu.SemaphoreType.DMA((2,)),
             pltpu.SemaphoreType.DMA((SWEEPS, 4)),
             pltpu.SemaphoreType.DMA((SWEEPS, 4)),
             pltpu.SemaphoreType.DMA,
@@ -580,6 +601,28 @@
         vertex,
         count,
     )
+    return pl.pallas_call(
+        vertex_sums,
+        out_shape=(
+            jax.ShapeDtypeStruct((5, 32, 1024), F32),
+            jax.ShapeDtypeStruct((3, VERT_DEV), F32),
+        ),
+        in_specs=[pl.BlockSpec(memory_space=pl.ANY)] * 2,
+        out_specs=(
+            pl.BlockSpec(memory_space=pl.ANY),
+            pl.BlockSpec(memory_space=pltpu.VMEM),
+        ),
+        scratch_shapes=[
+            vmem((4, blocks, LANES), F32),
+            vmem((5, 32, 1024), F32),
+            vmem((96, slots * 4), BF16),
+            vmem((128, slots * 4), BF16),
+            pltpu.SemaphoreType.DMA,
+            pltpu.SemaphoreType.DMA((5,)),
+            pltpu.SemaphoreType.DMA((5,)),
+        ],
+        compiler_params=pltpu.CompilerParams(vmem_limit_bytes=60 * 1024 * 1024),
+    )(adjoint, received)
 
 
 def solution(mesh):

time: 39 us -> 34.5 us (0.88)
  local copies, waits for them, and re-layouts: 2.6 us -> 0 us
  Pallas kernels: 35.6 us -> 33.7 us
    pallas_call x1, Pallas kernels: 35.6 us -> 29.8 us  [local(): pl.pallas_call(functools.partial(kernel, groups, blocks), out_shape=(jax....]
    pallas_call x0 -> x1, Pallas kernels: none -> 3.89 us  [local(): pl.pallas_call(vertex_sums, out_shape=(jax.ShapeDtypeStruct((5, 32, 1024)...]
    unnamed x4 -> x0, local copies, waits for them, and re-layouts: 2.6 us -> none
where the time goes in v2:
time: 34.5 us; the launch traced here: 34.3 us
  Pallas kernels  33.7 us (98%)
  between operations  0.64 us (2%)
    pallas_call x1, Pallas kernels, local(): pl.pallas_call(functools.partial(kernel, groups, blocks), out_shape=(jax....  29.8 us
    pallas_call x1, Pallas kernels, local(): pl.pallas_call(vertex_sums, out_shape=(jax.ShapeDtypeStruct((5, 32, 1024)...  3.89 us

profile of v2, /device:TPU:1, one launch (start us, length us, event | category | flops | bytes accessed | tf_op | source)
XLA Modules:
  0.0 34.3 jit_solution(8506945132113211478)
XLA Ops:
  0.6 29.8 %shard_map.113 = (f32[5,32,1024]{2,1,0:T(8,128)}, f32[4,64,128]{2,1,0:T(8,128)}) custom-call(f32[5,32,1024]{2,1,0:T(8,128)} %init_hbm.1, f32[5,32,1024]{2,1,0:T(8,128)} %rhs_hbm.1, f32[5,32,1024]{2,1,0:T(8,128)} %flow_hbm.1, bf16[6,32,1024]{2,1,0:T(8,128)(2,1)} %face_hbm.1, f32[32,1024]{1,0:T(8,128)} %pseudo_hbm.1, f32[3,4,2048]{2,1,0:T(4,128)} %bitcast.2, ...), custom_call_target="tpu_custom_call" | custom-call | tf_op jit(solution)/shard_map/pallas_call | solution.py:547
  30.5 3.9 %shard_map.114 = (f32[5,32,1024]{2,1,0:T(8,128)}, f32[3,1536]{1,0:T(4,128)}) custom-call(f32[5,32,1024]{2,1,0:T(8,128)} %get-tuple-element.4.adj, f32[4,64,128]{2,1,0:T(8,128)} %get-tuple-element.5.recv_hbm), custom_call_target="tpu_custom_call" | custom-call | tf_op jit(solution)/shard_map/pallas_call | solution.py:604

commit v3 on v2

--- a/solution.py
+++ b/solution.py
@@ -7,9 +7,9 @@
 from jax.experimental.pallas import tpu as pltpu
 from jax.sharding import PartitionSpec as P
 
-SWEEPS = 2
 VERT_DEV = 1536
 CAP = 32
+PLANES = 17
 LANES = 128
 GAMMA = 1.4
 LOCAL = 8
@@ -65,8 +65,10 @@
     scaled,
     coef,
     press,
-    y_send,
-    y_recv,
+    face_send,
+    face_recv,
+    edge_send,
+    edge_recv,
     table,
     onehot,
     found,
@@ -83,6 +85,24 @@
     block = lax.axis_index("blk")
     columns = 8
     chunks = blocks // 8
+
+    def loaded(*wanted):
+        for position, (source, target) in enumerate(loads):
+            if any(target is one for one in wanted):
+                pltpu.make_async_copy(source, target, load_sem.at[position]).wait()
+
+    def inner(ref):
+        return ref.at[:, pl.ds(1, columns), pl.ds(8, 32), :]
+
+    grp_up = {"grp": lax.rem(group + 1, groups)}
+    grp_down = {"grp": lax.rem(group + groups - 1, groups)}
+    blk_up = {"blk": lax.rem(block + 1, blocks)}
+    blk_down = {"blk": lax.rem(block + blocks - 1, blocks)}
+
+    barrier = pltpu.get_barrier_semaphore()
+    diagonals = [[{**one, **two} for two in (blk_down, blk_up)] for one in (grp_down, grp_up)]
+    for device in [grp_up, grp_down, blk_up, blk_down] + diagonals[0] + diagonals[1]:
+        pl.semaphore_signal(barrier, inc=1, device_id=device, device_id_type=MESH)
 
     loads = [
         (flow_hbm, flow),
@@ -104,23 +124,6 @@
     for position, (source, target) in enumerate(loads):
         pltpu.make_async_copy(source, target, load_sem.at[position]).start()
 
-    def loaded(*wanted):
-        for position, (source, target) in enumerate(loads):
-            if any(target is one for one in wanted):
-                pltpu.make_async_copy(source, target, load_sem.at[position]).wait()
-
-    def inner(ref):
-        return ref.at[:, pl.ds(1, columns), pl.ds(8, 32), :]
-
-    grp_up = {"grp": lax.rem(group + 1, groups)}
-    grp_down = {"grp": lax.rem(group + groups - 1, groups)}
-    blk_up = {"blk": lax.rem(block + 1, blocks)}
-    blk_down = {"blk": lax.rem(block + blocks - 1, blocks)}
-
-    barrier = pltpu.get_barrier_semaphore()
-    for device in (grp_up, grp_down):
-        pl.semaphore_signal(barrier, inc=1, device_id=device, device_id_type=MESH)
-
     def greet(step, carry):
         pl.semaphore_signal(
             barrier,
@@ -130,51 +133,139 @@
         )
         return carry
 
-    lax.fori_loop(1, blocks, greet, 0)
+    lax.fori_loop(2, blocks - 1, greet, 0)
 
     tile_lane = lane_iota((8, LANES))
+    tile_row = row_iota((8, LANES))
     lane_block = tile_lane // CAP
 
-    def halo_copies(adj, sweep):
-        span = pl.ds(1, columns)
+    first_end = (tile_row == 0) & (lane_block == 0)
+    last_end = (tile_row == 7) & (lane_block == 3)
+
+    def take_plane(read, side):
+        if side < 2:
+            row = 31 * side
+            return jnp.concatenate([read(tile, row, 1) for tile in range(columns)], axis=0)
+        tile, home = ((0, 0), (columns - 1, 3))[side - 2]
+        total = None
+        for part in range(4):
+            value = read(tile, 8 * part, 8)
+            turn = (part - home) % 4 * CAP
+            if turn:
+                value = pltpu.roll(value, turn, 1)
+            total = value if total is None else jnp.where(lane_block == part, value, total)
+        return total
+
+    def in_adjoint(adj, field):
+        return lambda tile, row, count: adj[field, tile + 1, pl.ds(8 + row, count), :]
+
+    def in_table(ref, place):
+        return lambda tile, row, count: ref[place, tile, pl.ds(row, count), :]
+
+    def fill_face(side):
+        for f in range(5):
+            face_send[side, f] = take_plane(in_adjoint(adj_a, f), side)
+            face_send[side, 5 + f] = take_plane(in_adjoint(adj_b, f), side)
+            face_send[side, 10 + f] = take_plane(in_table(coef, (0, 1, 2, 4, 5)[f]), side)
+        outward = 2 * (side // 2) + 1 - side % 2
+        along = 2 - 2 * (side // 2)
+        face_send[side, 15] = take_plane(in_table(gface, outward), side)
+        face_send[side, 16] = jnp.where(
+            first_end,
+            take_plane(in_table(gface, along + 1), side),
+            jnp.where(last_end, take_plane(in_table(gface, along), side), 0.0),
+        )
+
+    def fill_edge(upper_x, upper_y):
+        tile, home = ((1, 0), (columns, 3))[upper_y]
+        row = 8 + 31 * upper_x
+        lines = [adj_a[f, tile, pl.ds(row, 1), :] for f in range(5)]
+        value = jnp.concatenate(lines + [jnp.zeros((3, LANES), F32)], axis=0)
+        value = jnp.where(lane_block == home, value, 0.0)
+        value = value + pltpu.roll(value, CAP, 1)
+        edge_send[upper_x, upper_y] = value + pltpu.roll(value, 2 * CAP, 1)
+
+    def halo_copies():
         parts = [
-            (adj.at[:, span, pl.ds(39, 1), :], adj.at[:, span, pl.ds(7, 1), :], grp_up),
-            (adj.at[:, span, pl.ds(8, 1), :], adj.at[:, span, pl.ds(40, 1), :], grp_down),
-            (y_send.at[sweep, 0], y_recv.at[sweep, 0], blk_up),
-            (y_send.at[sweep, 1], y_recv.at[sweep, 1], blk_down),
+            (face_send.at[side], face_recv.at[side + 1 - 2 * (side % 2)], device)
+            for side, device in enumerate((grp_down, grp_up, blk_down, blk_up))
+        ] + [
+            (edge_send.at[i, j], edge_recv.at[1 - i, 1 - j], diagonals[i][j])
+            for i in range(2)
+            for j in range(2)
         ]
         return [
             pltpu.make_async_remote_copy(
                 src_ref=source,
                 dst_ref=target,
-                send_sem=halo_send.at[sweep, position],
-                recv_sem=halo_recv.at[sweep, position],
+                send_sem=halo_send.at[position],
+                recv_sem=halo_recv.at[position],
                 device_id=device,
                 device_id_type=MESH,
             )
             for position, (source, target, device) in enumerate(parts)
         ]
 
-    def pack(adj, sweep):
-        for field in range(5):
-            for side, tile, home in ((0, columns, 3), (1, 1, 0)):
-                total = None
+    def one_way(faces_of, side, axis, sign, weight, value):
+        velocity = [faces_of[side, 10 + k] for k in range(3)]
+        enthalpy = faces_of[side, 13]
+        reach = faces_of[side, 14]
+        half_sq = (0.5 * (GAMMA - 1.0)) * (
+            velocity[0] * velocity[0] + velocity[1] * velocity[1] + velocity[2] * velocity[2]
+        )
+        speed = velocity[axis]
+        dot = (
+            velocity[0] * value[1]
+            + velocity[1] * value[2]
+            + velocity[2] * value[3]
+            + enthalpy * value[4]
+        )
+        turned = value[1 + axis] + speed * value[4]
+        scaled_turn = (GAMMA - 1.0) * turned
+        result = [half_sq * turned - speed * dot]
+        for k in range(3):
+            entry = speed * value[1 + k] - scaled_turn * velocity[k]
+            result.append(entry + value[0] + dot if k == axis else entry)
+        result.append(scaled_turn + speed * value[4])
+        steady, signed = weight * reach, weight * sign
+        return [signed * result[f] + steady * value[f] for f in range(5)]
+
+    def complete(side):
+        axis, cross_axis = side // 2, 1 - side // 2
+        sign = 2.0 * (side % 2) - 1.0
+        mine = [face_send[side, f] for f in range(5)]
+        theirs = [face_recv[side, f] for f in range(5)]
+        gain = one_way(face_send, side, axis, sign, face_send[side, 15], theirs)
+        outer = one_way(face_recv, side, axis, -sign, face_recv[side, 15], mine)
+        if side < 2:
+            ends = edge_recv[side, 0], edge_recv[side, 1]
+        else:
+            ends = edge_recv[0, side - 2], edge_recv[1, side - 2]
+        corner = [
+            jnp.where(last_end, ends[1][f : f + 1], jnp.where(first_end, ends[0][f : f + 1], 0.0))
+            for f in range(5)
+        ]
+        end_sign = jnp.where(last_end, 1.0, -1.0)
+        extra = one_way(face_recv, side, cross_axis, end_sign, face_recv[side, 16], corner)
+        for f in range(5):
+            halo = face_recv[side, 5 + f] + outer[f] + extra[f]
+            if side < 2:
+                own_row, halo_row = ((8, 7), (39, 40))[side]
+                for tile in range(columns):
+                    adj_b[f, 1 + tile, pl.ds(halo_row, 1), :] = halo[tile : tile + 1]
+                    adj_b[f, 1 + tile, pl.ds(own_row, 1), :] = (
+                        adj_b[f, 1 + tile, pl.ds(own_row, 1), :] + gain[f][tile : tile + 1]
+                    )
+            else:
+                tile, home, halo_tile, halo_home = ((1, 0, 0, 3), (columns, 3, columns + 1, 0))[side - 2]
                 for part in range(4):
-                    value = adj[field, tile, pl.ds(8 + 8 * part, 8), :]
-                    turn = (part - home) % 4 * CAP
-                    if turn:
-                        value = pltpu.roll(value, turn, 1)
-                    total = value if total is None else jnp.where(lane_block == part, value, total)
-                y_send[sweep, side, field] = total
-
-    def unpack(adj, sweep):
-        for field in range(5):
-            for side, tile, home in ((0, 0, 3), (1, columns + 1, 0)):
-                value = y_recv[sweep, side, field]
-                for part in range(4):
+                    rows = pl.ds(8 + 8 * part, 8)
+                    turn = (halo_home - part) % 4 * CAP
+                    adj_b[f, halo_tile, rows, :] = pltpu.roll(halo, turn, 1) if turn else halo
                     turn = (home - part) % 4 * CAP
-                    adj[field, tile, pl.ds(8 + 8 * part, 8), :] = (
-                        pltpu.roll(value, turn, 1) if turn else value
+                    moved = pltpu.roll(gain[f], turn, 1) if turn else gain[f]
+                    adj_b[f, tile, rows, :] = adj_b[f, tile, rows, :] + jnp.where(
+                        lane_block == home, moved, 0.0
                     )
 
     def sweep_tile(source, store, tile, part):
@@ -247,35 +338,22 @@
     def store_c(f, tile, part, value):
         adj_c[f, pl.ds(8 * part, 8), pl.ds(pl.multiple_of(tile * LANES, LANES), LANES)] = value
 
-    def interior(source, store):
+    def sweep(source, store):
         def body(tile, carry):
-            for part in (1, 2):
+            for part in range(4):
                 sweep_tile(source, store, tile, part)
             return carry
 
-        lax.fori_loop(1, columns - 1, body, 0, unroll=4)
-
-    def boundary(source, store):
-        def body(tile, carry):
-            for part in (0, 3):
-                sweep_tile(source, store, tile, part)
-            return carry
-
-        lax.fori_loop(0, columns, body, 0, unroll=4)
-
-        def ends(step, carry):
-            for part in (1, 2):
-                sweep_tile(source, store, step * (columns - 1), part)
-            return carry
-
-        lax.fori_loop(0, 2, ends, 0)
-
-    pltpu.make_async_copy(inner(adj_a), inner(adj_a), load_sem.at[len(loads)]).wait()
-    pack(adj_a, 0)
-    pl.semaphore_wait(barrier, blocks + 1)
-    first_halo = halo_copies(adj_a, 0)
-    for copy in first_halo:
-        copy.start()
+        lax.fori_loop(0, columns, body, 0, unroll=2)
+
+    nothing = jnp.zeros((8, LANES), F32)
+    for f in range(5):
+        for tile in range(columns):
+            adj_a[f, 1 + tile, pl.ds(0, 8), :] = nothing
+            adj_a[f, 1 + tile, pl.ds(40, 8), :] = nothing
+        for part in range(4):
+            adj_a[f, 0, pl.ds(8 + 8 * part, 8), :] = nothing
+            adj_a[f, columns + 1, pl.ds(8 + 8 * part, 8), :] = nothing
 
     loaded(flow, face, pseudo, rhs)
     tall_row = row_iota((16, LANES))
@@ -324,17 +402,18 @@
         return carry
 
     lax.fori_loop(0, 2 * columns, coefficients, 0, unroll=2)
-    interior(adj_a, store_b)
-    for copy in first_halo:
-        copy.wait_recv()
-    unpack(adj_a, 0)
-    boundary(adj_a, store_b)
-
-    pack(adj_b, 1)
-    second_halo = halo_copies(adj_b, 1)
-    for copy in second_halo:
+    pltpu.make_async_copy(inner(adj_a), inner(adj_a), load_sem.at[len(loads)]).wait()
+    sweep(adj_a, store_b)
+
+    for side in range(4):
+        fill_face(side)
+    for i in range(2):
+        for j in range(2):
+            fill_edge(i, j)
+    pl.semaphore_wait(barrier, blocks + 5)
+    halo = halo_copies()
+    for copy in halo:
         copy.start()
-    interior(adj_b, store_c)
 
     loaded(cell, coords, weights, vertex, count)
 
@@ -348,7 +427,6 @@
 
     lax.fori_loop(0, chunks, pick_cells, 0)
 
-    tile_row = row_iota((8, LANES))
     own_block = lane_block == tile_row % 4
     upper_half = tile_row < 4
     slot = tile_lane % CAP
@@ -402,10 +480,11 @@
 
     lax.fori_loop(0, chunks, geometry, 0, unroll=4)
 
-    for copy in second_halo:
+    for copy in halo:
         copy.wait_recv()
-    unpack(adj_b, 1)
-    boundary(adj_b, store_c)
+    for side in range(4):
+        complete(side)
+    sweep(adj_b, store_c)
     adj_copy = pltpu.make_async_copy(adj_c, adj_out, out_sem.at[0])
     adj_copy.start()
 
@@ -450,20 +529,18 @@
     planes = blocks // LOCAL
     z, x, core = block // LOCAL, block % LOCAL // 2, block % 2
 
-    def partner(step):
-        far = step // LOCAL
-        near = step % LOCAL
-        return (
+    def post(step, carry):
+        turn = step // LOCAL
+        far = planes // 2 + (1 - 2 * (turn % 2)) * ((turn + 1) // 2)
+        near = LOCAL - 1 - step % LOCAL
+        owner = (
             lax.rem(z + far, planes) * LOCAL
             + lax.rem(x + near // 2, 4) * 2
             + lax.rem(core + near % 2, 2)
         )
-
-    def post(step, carry):
-        owner = partner(step)
         pltpu.make_async_remote_copy(
             src_ref=send.at[:, pl.ds(owner, 1), :],
-            dst_ref=recv.at[:, pl.ds(step - 1, 1), :],
+            dst_ref=recv.at[:, pl.ds(step, 1), :],
             send_sem=term_send,
             recv_sem=term_recv,
             device_id={"blk": owner},
@@ -471,7 +548,7 @@
         ).start()
         return carry
 
-    lax.fori_loop(1, blocks, post, 0)
+    lax.fori_loop(0, blocks - 1, post, 0)
     own = pltpu.make_async_copy(
         send.at[:, pl.ds(block, 1), :], recv.at[:, pl.ds(blocks - 1, 1), :], out_sem.at[1]
     )
@@ -487,7 +564,7 @@
     others.wait_recv()
     own.wait()
 
-    for copy in first_halo + second_halo:
+    for copy in halo:
         copy.wait_send()
     others.wait_send()
     adj_copy.wait()
@@ -572,8 +649,10 @@
             vmem((5, 8, 32, LANES), F32),
             vmem((6, 8, 32, LANES), F32),
             vmem((8, 32, LANES), F32),
-            vmem((SWEEPS, 2, 5, 8, LANES), F32),
-            vmem((SWEEPS, 2, 5, 8, LANES), F32),
+            vmem((4, PLANES, 8, LANES), F32),
+            vmem((4, PLANES, 8, LANES), F32),
+            vmem((2, 2, 8, LANES), F32),
+            vmem((2, 2, 8, LANES), F32),
             vmem((256, 1024), BF16),
             vmem((1024, slots), BF16),
             vmem((256, slots), F32),
@@ -581,8 +660,8 @@
             vmem((4, blocks, LANES), F32),
             pltpu.SemaphoreType.DMA((10,)),
             pltpu.SemaphoreType.DMA((2,)),
-            pltpu.SemaphoreType.DMA((SWEEPS, 4)),
-            pltpu.SemaphoreType.DMA((SWEEPS, 4)),
+            pltpu.SemaphoreType.DMA((8,)),
+            pltpu.SemaphoreType.DMA((8,)),
             pltpu.SemaphoreType.DMA,
             pltpu.SemaphoreType.DMA,
         ],

time: 34.5 us -> 32 us (0.928)
  Pallas kernels: 33.7 us -> 31.2 us
    pallas_call x1, Pallas kernels: 29.8 us -> 27.4 us  [local(): pl.pallas_call(functools.partial(kernel, groups, blocks), out_shape=(jax....]
where the time goes in v3:
time: 32 us; the launch traced here: 31.9 us
  Pallas kernels  31.2 us (98%)
  between operations  0.64 us (2%)
    pallas_call x1, Pallas kernels, local(): pl.pallas_call(functools.partial(kernel, groups, blocks), out_shape=(jax....  27.4 us
    pallas_call x1, Pallas kernels, local(): pl.pallas_call(vertex_sums, out_shape=(jax.ShapeDtypeStruct((5, 32, 1024)...  3.89 us

profile of v3, /device:TPU:1, one launch (start us, length us, event | category | flops | bytes accessed | tf_op | source)
XLA Modules:
  0.0 31.9 jit_solution(5685151459189970983)
XLA Ops:
  0.6 27.4 %shard_map.113 = (f32[5,32,1024]{2,1,0:T(8,128)}, f32[4,64,128]{2,1,0:T(8,128)}) custom-call(f32[5,32,1024]{2,1,0:T(8,128)} %init_hbm.1, f32[5,32,1024]{2,1,0:T(8,128)} %rhs_hbm.1, f32[5,32,1024]{2,1,0:T(8,128)} %flow_hbm.1, bf16[6,32,1024]{2,1,0:T(8,128)(2,1)} %face_hbm.1, f32[32,1024]{1,0:T(8,128)} %pseudo_hbm.1, f32[3,4,2048]{2,1,0:T(4,128)} %bitcast.2, ...), custom_call_target="tpu_custom_call" | custom-call | tf_op jit(solution)/shard_map/pallas_call | solution.py:624
  28.0 3.9 %shard_map.114 = (f32[5,32,1024]{2,1,0:T(8,128)}, f32[3,1536]{1,0:T(4,128)}) custom-call(f32[5,32,1024]{2,1,0:T(8,128)} %get-tuple-element.4.adj, f32[4,64,128]{2,1,0:T(8,128)} %get-tuple-element.5.recv_hbm), custom_call_target="tpu_custom_call" | custom-call | tf_op jit(solution)/shard_map/pallas_call | solution.py:683

commit v4 on v3

--- a/solution.py
+++ b/solution.py
@@ -80,6 +80,7 @@
     halo_recv,
     term_send,
     term_recv,
+    plane_sem,
 ):
     group = lax.axis_index("grp")
     block = lax.axis_index("blk")
@@ -124,16 +125,16 @@
     for position, (source, target) in enumerate(loads):
         pltpu.make_async_copy(source, target, load_sem.at[position]).start()
 
-    def greet(step, carry):
-        pl.semaphore_signal(
-            barrier,
-            inc=1,
-            device_id={"blk": lax.rem(block + step, blocks)},
-            device_id_type=MESH,
-        )
-        return carry
-
-    lax.fori_loop(2, blocks - 1, greet, 0)
+    planes = blocks // LOCAL
+    z, x, core = block // LOCAL, block % LOCAL // 2, block % 2
+    for step in range(1, LOCAL):
+        beside = z * LOCAL + lax.rem(x + step // 2, 4) * 2 + lax.rem(core + step % 2, 2)
+        pl.semaphore_signal(barrier, inc=1, device_id={"blk": beside}, device_id_type=MESH)
+    column = [
+        {"blk": lax.rem(z + step, planes) * LOCAL + block % LOCAL} for step in range(1, planes)
+    ]
+    for device in column:
+        pl.semaphore_signal(barrier, inc=1, device_id=device, device_id_type=MESH)
 
     tile_lane = lane_iota((8, LANES))
     tile_row = row_iota((8, LANES))
@@ -410,10 +411,12 @@
     for i in range(2):
         for j in range(2):
             fill_edge(i, j)
-    pl.semaphore_wait(barrier, blocks + 5)
+    pl.semaphore_wait(barrier, 8 + LOCAL - 1 + planes - 1)
     halo = halo_copies()
     for copy in halo:
         copy.start()
+    for device in column:
+        pl.semaphore_signal(plane_sem, inc=1, device_id=device, device_id_type=MESH)
 
     loaded(cell, coords, weights, vertex, count)
 
@@ -526,8 +529,8 @@
 
     lax.fori_loop(0, chunks, terms, 0, unroll=8)
 
-    planes = blocks // LOCAL
-    z, x, core = block // LOCAL, block % LOCAL // 2, block % 2
+    if planes > 1:
+        pl.semaphore_wait(plane_sem, planes - 1)
 
     def post(step, carry):
         turn = step // LOCAL
@@ -587,6 +590,9 @@
     recv_copy.wait()
     chunks = recv.shape[1] // 8
 
+    bands = [(row_iota((16, LANES)) + 16 * band).astype(F32).astype(BF16) for band in range(8)]
+    one, zero = jnp.ones((16, LANES), BF16), jnp.zeros((16, LANES), BF16)
+
     def operands(chunk, carry):
         rows = pl.ds(pl.multiple_of(chunk * 8, 8), 8)
         vertices = recv[3, rows, :].astype(jnp.int32)
@@ -599,7 +605,9 @@
             halves += [high, value - high]
         for s in range(8):
             lanes = pl.ds(pl.multiple_of(chunk * 1024 + s * LANES, LANES), LANES)
-            right_op[:, lanes] = jnp.where(row_iota((128, LANES)) == minor[s : s + 1], 1.0, 0.0).astype(BF16)
+            low = jnp.broadcast_to(minor[s : s + 1].astype(F32), (16, LANES)).astype(BF16)
+            for band in range(8):
+                right_op[pl.ds(16 * band, 16), lanes] = jnp.where(low == bands[band], one, zero)
             hit = row_iota((16, LANES)) == major[s : s + 1]
             for n, value in enumerate(halves):
                 left_op[pl.ds(16 * n, 16), lanes] = jnp.where(hit, value[s : s + 1], 0.0).astype(BF16)
@@ -664,6 +672,7 @@
             pltpu.SemaphoreType.DMA((8,)),
             pltpu.SemaphoreType.DMA,
             pltpu.SemaphoreType.DMA,
+            pltpu.SemaphoreType.REGULAR,
         ],
         compiler_params=pltpu.CompilerParams(
             collective_id=0, has_side_effects=True, vmem_limit_bytes=60 * 1024 * 1024

time: 32 us -> 30.7 us (0.959)
  Pallas kernels: 31.2 us -> 29.9 us
    pallas_call x1, Pallas kernels: 27.4 us -> 26.2 us  [local(): pl.pallas_call(functools.partial(kernel, groups, blocks), out_shape=(jax....]
where the time goes in v4:
time: 30.7 us; the launch traced here: 30.6 us
  Pallas kernels  29.9 us (97%)
  between operations  0.64 us (2%)
    pallas_call x1, Pallas kernels, local(): pl.pallas_call(functools.partial(kernel, groups, blocks), out_shape=(jax....  26.2 us
    pallas_call x1, Pallas kernels, local(): pl.pallas_call(vertex_sums, out_shape=(jax.ShapeDtypeStruct((5, 32, 1024)...  3.73 us

profile of v4, /device:TPU:1, one launch (start us, length us, event | category | flops | bytes accessed | tf_op | source)
XLA Modules:
  0.0 30.6 jit_solution(5727130479681637886)
XLA Ops:
  0.6 26.2 %shard_map.113 = (f32[5,32,1024]{2,1,0:T(8,128)}, f32[4,64,128]{2,1,0:T(8,128)}) custom-call(f32[5,32,1024]{2,1,0:T(8,128)} %init_hbm.1, f32[5,32,1024]{2,1,0:T(8,128)} %rhs_hbm.1, f32[5,32,1024]{2,1,0:T(8,128)} %flow_hbm.1, bf16[6,32,1024]{2,1,0:T(8,128)(2,1)} %face_hbm.1, f32[32,1024]{1,0:T(8,128)} %pseudo_hbm.1, f32[3,4,2048]{2,1,0:T(4,128)} %bitcast.2, ...), custom_call_target="tpu_custom_call" | custom-call | tf_op jit(solution)/shard_map/pallas_call | solution.py:632
  26.8 3.7 %shard_map.114 = (f32[5,32,1024]{2,1,0:T(8,128)}, f32[3,1536]{1,0:T(4,128)}) custom-call(f32[5,32,1024]{2,1,0:T(8,128)} %get-tuple-element.4.adj, f32[4,64,128]{2,1,0:T(8,128)} %get-tuple-element.5.recv_hbm), custom_call_target="tpu_custom_call" | custom-call | tf_op jit(solution)/shard_map/pallas_call | solution.py:692

commit v5 on v4

--- a/solution.py
+++ b/solution.py
@@ -347,6 +347,25 @@
 
         lax.fori_loop(0, columns, body, 0, unroll=2)
 
+    def interior(source, store):
+        def body(tile, carry):
+            for part in (1, 2):
+                sweep_tile(source, store, tile, part)
+            return carry
+
+        lax.fori_loop(1, columns - 1, body, 0, unroll=3)
+
+    def boundary(source, store):
+        def body(tile, carry):
+            for part in (0, 3):
+                sweep_tile(source, store, tile, part)
+            return carry
+
+        lax.fori_loop(0, columns, body, 0, unroll=4)
+        for tile in (0, columns - 1):
+            for part in (1, 2):
+                sweep_tile(source, store, tile, part)
+
     nothing = jnp.zeros((8, LANES), F32)
     for f in range(5):
         for tile in range(columns):
@@ -406,17 +425,22 @@
     pltpu.make_async_copy(inner(adj_a), inner(adj_a), load_sem.at[len(loads)]).wait()
     sweep(adj_a, store_b)
 
-    for side in range(4):
-        fill_face(side)
     for i in range(2):
         for j in range(2):
             fill_edge(i, j)
+    for side in (2, 3):
+        fill_face(side)
     pl.semaphore_wait(barrier, 8 + LOCAL - 1 + planes - 1)
     halo = halo_copies()
-    for copy in halo:
+    for copy in halo[4:] + halo[2:4]:
         copy.start()
+    for side in (0, 1):
+        fill_face(side)
+        halo[side].start()
     for device in column:
         pl.semaphore_signal(plane_sem, inc=1, device_id=device, device_id_type=MESH)
+
+    interior(adj_b, store_c)
 
     loaded(cell, coords, weights, vertex, count)
 
@@ -487,7 +511,7 @@
         copy.wait_recv()
     for side in range(4):
         complete(side)
-    sweep(adj_b, store_c)
+    boundary(adj_b, store_c)
     adj_copy = pltpu.make_async_copy(adj_c, adj_out, out_sem.at[0])
     adj_copy.start()
 
@@ -594,7 +618,7 @@
     one, zero = jnp.ones((16, LANES), BF16), jnp.zeros((16, LANES), BF16)
 
     def operands(chunk, carry):
-        rows = pl.ds(pl.multiple_of(chunk * 8, 8), 8)
+        rows = pl.ds(chunk * 8, 8)
         vertices = recv[3, rows, :].astype(jnp.int32)
         major = jnp.right_shift(vertices, 7)
         minor = jnp.bitwise_and(vertices, 127)
@@ -604,7 +628,7 @@
             high = value.astype(BF16).astype(F32)
             halves += [high, value - high]
         for s in range(8):
-            lanes = pl.ds(pl.multiple_of(chunk * 1024 + s * LANES, LANES), LANES)
+            lanes = pl.ds(chunk * 1024 + s * LANES, LANES)
             low = jnp.broadcast_to(minor[s : s + 1].astype(F32), (16, LANES)).astype(BF16)
             for band in range(8):
                 right_op[pl.ds(16 * band, 16), lanes] = jnp.where(low == bands[band], one, zero)
@@ -613,10 +637,17 @@
                 left_op[pl.ds(16 * n, 16), lanes] = jnp.where(hit, value[s : s + 1], 0.0).astype(BF16)
         return carry
 
-    lax.fori_loop(0, chunks, operands, 0)
-    sums = lax.dot_general(
-        left_op[...], right_op[...], (((1,), (1,)), ((), ())), preferred_element_type=F32
-    )
+    sums = None
+    for chunk in range(chunks):
+        operands(chunk, 0)
+        lanes = pl.ds(chunk * 1024, 1024)
+        part = lax.dot_general(
+            left_op[:, lanes],
+            right_op[:, lanes],
+            (((1,), (1,)), ((), ())),
+            preferred_element_type=F32,
+        )
+        sums = part if sums is None else sums + part
     for k in range(3):
         both = sums[32 * k : 32 * k + 16] + sums[32 * k + 16 : 32 * k + 32]
         for h in range(VERT_DEV // LANES):

time: 30.7 us -> 29.4 us (0.958)
  Pallas kernels: 29.9 us -> 28.6 us
    pallas_call x1, Pallas kernels: 26.2 us -> 25.4 us  [local(): pl.pallas_call(functools.partial(kernel, groups, blocks), out_shape=(jax....]
    pallas_call x1, Pallas kernels: 3.73 us -> 3.16 us  [local(): pl.pallas_call(vertex_sums, out_shape=(jax.ShapeDtypeStruct((5, 32, 1024)...]
where the time goes in v5:
time: 29.4 us; the launch traced here: 29.2 us
  Pallas kernels  28.6 us (97%)
  between operations  0.64 us (2%)
    pallas_call x1, Pallas kernels, local(): pl.pallas_call(functools.partial(kernel, groups, blocks), out_shape=(jax....  25.4 us
    pallas_call x1, Pallas kernels, local(): pl.pallas_call(vertex_sums, out_shape=(jax.ShapeDtypeStruct((5, 32, 1024)...  3.16 us

profile of v5, /device:TPU:1, one launch (start us, length us, event | category | flops | bytes accessed | tf_op | source)
XLA Modules:
  0.0 29.2 jit_solution(8077766894258038187)
XLA Ops:
  0.6 25.4 %shard_map.113 = (f32[5,32,1024]{2,1,0:T(8,128)}, f32[4,64,128]{2,1,0:T(8,128)}) custom-call(f32[5,32,1024]{2,1,0:T(8,128)} %init_hbm.1, f32[5,32,1024]{2,1,0:T(8,128)} %rhs_hbm.1, f32[5,32,1024]{2,1,0:T(8,128)} %flow_hbm.1, bf16[6,32,1024]{2,1,0:T(8,128)(2,1)} %face_hbm.1, f32[32,1024]{1,0:T(8,128)} %pseudo_hbm.1, f32[3,4,2048]{2,1,0:T(4,128)} %bitcast.2, ...), custom_call_target="tpu_custom_call" | custom-call | tf_op jit(solution)/shard_map/pallas_call | solution.py:663
  26.1 3.2 %shard_map.114 = (f32[5,32,1024]{2,1,0:T(8,128)}, f32[3,1536]{1,0:T(4,128)}) custom-call(f32[5,32,1024]{2,1,0:T(8,128)} %get-tuple-element.4.adj, f32[4,64,128]{2,1,0:T(8,128)} %get-tuple-element.5.recv_hbm), custom_call_target="tpu_custom_call" | custom-call | tf_op jit(solution)/shard_map/pallas_call | solution.py:723

commit v6 on v5

--- a/solution.py
+++ b/solution.py
@@ -116,6 +116,8 @@
         (vertex_hbm, vertex),
         (count_hbm, count),
     ]
+    for position, (source, target) in enumerate(loads[:4]):
+        pltpu.make_async_copy(source, target, load_sem.at[position]).start()
     for tile in range(columns):
         pltpu.make_async_copy(
             init_hbm.at[:, :, pl.ds(tile * LANES, LANES)],
@@ -123,7 +125,8 @@
             load_sem.at[len(loads)],
         ).start()
     for position, (source, target) in enumerate(loads):
-        pltpu.make_async_copy(source, target, load_sem.at[position]).start()
+        if position >= 4:
+            pltpu.make_async_copy(source, target, load_sem.at[position]).start()
 
     planes = blocks // LOCAL
     z, x, core = block // LOCAL, block % LOCAL // 2, block % 2
@@ -345,7 +348,7 @@
                 sweep_tile(source, store, tile, part)
             return carry
 
-        lax.fori_loop(0, columns, body, 0, unroll=2)
+        lax.fori_loop(0, columns, body, 0, unroll=4)
 
     def interior(source, store):
         def body(tile, carry):

time: 29.4 us -> 29 us (0.986)
  Pallas kernels: 28.6 us -> 28.2 us
    pallas_call x1, Pallas kernels: 25.4 us -> 25.1 us  [local(): pl.pallas_call(functools.partial(kernel, groups, blocks), out_shape=(jax....]
where the time goes in v6:
time: 29 us; the launch traced here: 28.9 us
  Pallas kernels  28.2 us (97%)
  between operations  0.64 us (2%)
    pallas_call x1, Pallas kernels, local(): pl.pallas_call(functools.partial(kernel, groups, blocks), out_shape=(jax....  25.1 us
    pallas_call x1, Pallas kernels, local(): pl.pallas_call(vertex_sums, out_shape=(jax.ShapeDtypeStruct((5, 32, 1024)...  3.16 us

profile of v6, /device:TPU:1, one launch (start us, length us, event | category | flops | bytes accessed | tf_op | source)
XLA Modules:
  0.0 28.9 jit_solution(9309088947471624471)
XLA Ops:
  0.6 25.1 %shard_map.113 = (f32[5,32,1024]{2,1,0:T(8,128)}, f32[4,64,128]{2,1,0:T(8,128)}) custom-call(f32[5,32,1024]{2,1,0:T(8,128)} %init_hbm.1, f32[5,32,1024]{2,1,0:T(8,128)} %rhs_hbm.1, f32[5,32,1024]{2,1,0:T(8,128)} %flow_hbm.1, bf16[6,32,1024]{2,1,0:T(8,128)(2,1)} %face_hbm.1, f32[32,1024]{1,0:T(8,128)} %pseudo_hbm.1, f32[3,4,2048]{2,1,0:T(4,128)} %bitcast.2, ...), custom_call_target="tpu_custom_call" | custom-call | tf_op jit(solution)/shard_map/pallas_call | solution.py:666
  25.7 3.2 %shard_map.114 = (f32[5,32,1024]{2,1,0:T(8,128)}, f32[3,1536]{1,0:T(4,128)}) custom-call(f32[5,32,1024]{2,1,0:T(8,128)} %get-tuple-element.4.adj, f32[4,64,128]{2,1,0:T(8,128)} %get-tuple-element.5.recv_hbm), custom_call_target="tpu_custom_call" | custom-call | tf_op jit(solution)/shard_map/pallas_call | solution.py:726

commit v7 on v6

--- a/solution.py
+++ b/solution.py
@@ -534,16 +534,14 @@
 
     lax.fori_loop(0, 2 * columns, fill_table, 0)
 
-    found[...] = jnp.dot(table[...], onehot[...], preferred_element_type=F32)
-
-    def terms(chunk, carry):
+    def terms(chunk, place):
         lanes = pl.ds(pl.multiple_of(chunk * 256, 256), 256)
         rows = pl.ds(pl.multiple_of(chunk * 8, 8), 8)
         plane = jnp.right_shift(cell[:, lanes], 10)
         mine = row_iota((32, 256)) == plane
         fields = []
         for f in range(4):
-            value = found[32 * f : 32 * f + 32, lanes] + found[128 + 32 * f : 160 + 32 * f, lanes]
+            value = found[32 * f : 32 * f + 32, place] + found[128 + 32 * f : 160 + 32 * f, place]
             value = jnp.sum(jnp.where(mine, value, 0.0), axis=0, keepdims=True)
             fields.append(spread(value[:, :128], value[:, 128:]))
         b, a = fields[:3], fields[3]
@@ -552,33 +550,38 @@
         turn = cross(side, b)
         for k in range(3):
             send[k, rows, :] = a * gradient[k] + turn[k]
-        return carry
-
-    lax.fori_loop(0, chunks, terms, 0, unroll=8)
-
-    if planes > 1:
-        pl.semaphore_wait(plane_sem, planes - 1)
-
-    def post(step, carry):
-        turn = step // LOCAL
-        far = planes // 2 + (1 - 2 * (turn % 2)) * ((turn + 1) // 2)
-        near = LOCAL - 1 - step % LOCAL
-        owner = (
-            lax.rem(z + far, planes) * LOCAL
-            + lax.rem(x + near // 2, 4) * 2
-            + lax.rem(core + near % 2, 2)
+
+    pl.semaphore_wait(plane_sem, planes - 1)
+    for turn, far in enumerate((2, 1, 3, 0)):
+        pair = lax.rem(z // 2 + far, planes // 2)
+        found[:, pl.ds(turn * 512, 512)] = jnp.dot(
+            table[...],
+            onehot[:, pl.ds(pl.multiple_of(pair * 512, 512), 512)],
+            preferred_element_type=F32,
         )
-        pltpu.make_async_remote_copy(
-            src_ref=send.at[:, pl.ds(owner, 1), :],
-            dst_ref=recv.at[:, pl.ds(step, 1), :],
-            send_sem=term_send,
-            recv_sem=term_recv,
-            device_id={"blk": owner},
-            device_id_type=MESH,
-        ).start()
-        return carry
-
-    lax.fori_loop(0, blocks - 1, post, 0)
+        for half in range(2):
+            terms(2 * pair + half, pl.ds(turn * 512 + half * 256, 256))
+
+        def post(step, carry):
+            plane = 2 * pair + lax.rem(z + 1 - step // LOCAL, 2)
+            near = LOCAL - 1 - step % LOCAL
+            owner = (
+                plane * LOCAL
+                + lax.rem(x + near // 2, 4) * 2
+                + lax.rem(core + near % 2, 2)
+            )
+            away = lax.rem(plane - z + planes, planes)
+            pltpu.make_async_remote_copy(
+                src_ref=send.at[:, pl.ds(owner, 1), :],
+                dst_ref=recv.at[:, pl.ds(away * LOCAL + near - 1, 1), :],
+                send_sem=term_send,
+                recv_sem=term_recv,
+                device_id={"blk": owner},
+                device_id_type=MESH,
+            ).start()
+            return carry
+
+        lax.fori_loop(0, 2 * LOCAL - (far == 0), post, 0)
     own = pltpu.make_async_copy(
         send.at[:, pl.ds(block, 1), :], recv.at[:, pl.ds(blocks - 1, 1), :], out_sem.at[1]
     )

time: 29 us -> 28.7 us (0.990)
  no operation moved by 1% of the time
where the time goes in v7:
time: 28.7 us; the launch traced here: 28.6 us
  Pallas kernels  28 us (98%)
  between operations  0.64 us (2%)
    pallas_call x1, Pallas kernels, local(): pl.pallas_call(functools.partial(kernel, groups, blocks), out_shape=(jax....  24.8 us
    pallas_call x1, Pallas kernels, local(): pl.pallas_call(vertex_sums, out_shape=(jax.ShapeDtypeStruct((5, 32, 1024)...  3.16 us

profile of v7, /device:TPU:1, one launch (start us, length us, event | category | flops | bytes accessed | tf_op | source)
XLA Modules:
  0.0 28.6 jit_solution(16799450548159944101)
XLA Ops:
  0.6 24.8 %shard_map.113 = (f32[5,32,1024]{2,1,0:T(8,128)}, f32[4,64,128]{2,1,0:T(8,128)}) custom-call(f32[5,32,1024]{2,1,0:T(8,128)} %init_hbm.1, f32[5,32,1024]{2,1,0:T(8,128)} %rhs_hbm.1, f32[5,32,1024]{2,1,0:T(8,128)} %flow_hbm.1, bf16[6,32,1024]{2,1,0:T(8,128)(2,1)} %face_hbm.1, f32[32,1024]{1,0:T(8,128)} %pseudo_hbm.1, f32[3,4,2048]{2,1,0:T(4,128)} %bitcast.2, ...), custom_call_target="tpu_custom_call" | custom-call | tf_op jit(solution)/shard_map/pallas_call | solution.py:669
  25.5 3.2 %shard_map.114 = (f32[5,32,1024]{2,1,0:T(8,128)}, f32[3,1536]{1,0:T(4,128)}) custom-call(f32[5,32,1024]{2,1,0:T(8,128)} %get-tuple-element.4.adj, f32[4,64,128]{2,1,0:T(8,128)} %get-tuple-element.5.recv_hbm), custom_call_target="tpu_custom_call" | custom-call | tf_op jit(solution)/shard_map/pallas_call | solution.py:729
